TPU v7x, 256 devices: a whole 4x4x8 slice. The times are simulated.
256 devices in a mesh: dp: 256 (over y, z, x, core).
Axes of the slice: x: 4, y: 4, z: 8, core: 2. Of those that a mesh axis runs over, the one named last changes fastest.
Arguments:
- queries: bfloat16 [2048, 32, 128], P('dp')
- pages: bfloat16 [512, 1030, 128], P('dp')
- counts: int32 [512], P('dp'), may hold values from 700 to 1030
- labels: int32 [2048], P('dp'), may hold values from 0 to 511, as said below
- logit_scale: float32 [], replicated, may hold values from 0.02 to 0.1
- logit_bias: float32 [], replicated, may hold values from -6 to -1
Outputs:
- loss_total: float32 [], replicated
- grad_queries: float32 [2048, 32, 128], P('dp')
- grad_pages: float32 [512, 1030, 128], P('dp')
Inputs may be any that keep to these rules, and one draw needn't show every extreme that they name: `labels`: each query's positive page is one of the pages it is scored with.
All inputs are finite; a program needn't handle non-finite values.
Results may differ from a plain program's by a relative error of at most 0.0028.
Values may be sent and summed in bfloat16 or wider, within the bound.
A program may use at most 64 MiB of HBM per device.

v0:
```python
import jax
import jax.numpy as jnp
from jax import lax
from jax.sharding import PartitionSpec as P

ROUNDS = 4


SOFTMAX_WARMTH = 0.1


def partner_2(block, axis, bit):
    count = lax.axis_size(axis)
    route = []
    for low in range(count):
        high = low | 1 << bit
        if high != low and high < count:
            route += [(low, high), (high, low)]
    return lax.ppermute(block, axis, route)


def block_terms(query_block, page_block, page_mask, targets, logit_scale, logit_bias):
    n_query, q_tok, emb_width = query_block.shape
    flat_query = query_block.reshape(n_query * q_tok, emb_width)
    match_scores = lax.dot_general(
        page_block, flat_query, (((2,), (1,)), ((), ())), preferred_element_type=jnp.float32
    )
    match_scores = jnp.swapaxes(match_scores, 1, 2)
    retained_mask = page_mask[:, None, :] > 0
    row_maximum = jnp.max(jnp.where(retained_mask, match_scores, -jnp.inf), axis=2, keepdims=True)
    power_term = jnp.where(
        retained_mask, jnp.exp((match_scores - row_maximum) / SOFTMAX_WARMTH), 0.0
    )
    row_summation = jnp.sum(power_term, axis=2, keepdims=True)
    weights = power_term / row_summation
    smoothed_maximum = row_maximum[:, :, 0] + SOFTMAX_WARMTH * jnp.log(row_summation[:, :, 0])
    page_local = page_block.shape[0]
    page_score = jnp.sum(smoothed_maximum.reshape(page_local, n_query, q_tok), axis=2)
    logits_now = logit_scale * page_score + logit_bias
    sign_vals = 2.0 * targets.T - 1.0
    pair_loss = jnp.sum(jax.nn.softplus(-sign_vals * logits_now))
    slopes = -sign_vals * logit_scale * jax.nn.sigmoid(-sign_vals * logits_now)
    coefficient = (weights * jnp.repeat(slopes, q_tok, axis=1)[:, :, None]).astype(jnp.bfloat16)
    grad_rows = lax.dot_general(
        coefficient, page_block, (((0, 2), (0, 1)), ((), ())), preferred_element_type=jnp.float32
    )
    grad_page = lax.dot_general(
        coefficient, flat_query, (((1,), (0,)), ((), ())), preferred_element_type=jnp.float32
    )
    return (pair_loss, grad_rows.reshape(n_query, q_tok, emb_width), grad_page)


def per_device(queries, pages, counts, labels, logit_scale, logit_bias):
    log_count = lax.axis_size("dp").bit_length() - 1
    device = lax.axis_index("dp")
    page_local = pages.shape[0]
    page_len = pages.shape[1]
    positions = jnp.arange(page_len, dtype=jnp.int32)
    page_mask = (positions[None, :] < counts[:, None]).astype(jnp.bfloat16)
    offsets = jnp.arange(page_local, dtype=jnp.int32)

    def targets_for(partner):
        return (labels[:, None] == partner * page_local + offsets[None, :]).astype(jnp.float32)

    loss_sum, grad_query, grad_page = block_terms(
        queries, pages, page_mask, targets_for(device), logit_scale, logit_bias
    )
    for round_number in range(ROUNDS):
        bit_index = log_count - 1 - round_number
        partner = jnp.bitwise_xor(device, jnp.int32(1 << bit_index))
        far_pages, far_mask = partner_2((pages, page_mask), "dp", bit_index)
        block_loss, block_rows, far_grad = block_terms(
            queries, far_pages, far_mask, targets_for(partner), logit_scale, logit_bias
        )
        grad_query = grad_query + block_rows
        grad_page = grad_page + partner_2(far_grad, "dp", bit_index)
        loss_sum = loss_sum + block_loss
    summed_loss = lax.psum(loss_sum, "dp")
    return (summed_loss, grad_query, grad_page)


def solution(mesh):
    placed = (P("dp", None, None), P("dp", None, None), P("dp"), P("dp"), P(), P())
    return jax.shard_map(
        per_device,
        mesh=mesh,
        in_specs=placed,
        out_specs=(P(), P("dp", None, None), P("dp", None, None)),
        check_vma=False,
    )
```

profile of v0, /device:TPU:1, one launch (start us, length us, event | category | flops | bytes accessed | tf_op | source)
XLA Modules:
  0.0 291.0 jit_solution(6202191635378829655)
XLA Ops:
  0.6 0.8 compare_convert_fusion
  1.4 7.8 %collective-permute-start.4 = (bf16[2,1030]{1,0:T(2,128)(2,1)S(1)}, bf16[2,1030]{1,0:T(2,128)(2,1)S(1)}, u32[]{:S(2)}, u32[]{:S(2)}) collective-permute-start(bf16[2,1030]{1,0:T(2,128)(2,1)S(1)} %get-tuple-element.27), channel_id=1, source_target_pairs={{0,32},{32,0},{1,33},{33,1},{2,34},{34,2},{3,35},{35,3},{4,36},{36... | collective-permute-start | bytes 12368 | tf_op jit(solution)/shard_map/ppermute | solution.py:19
  9.2 1.3 collective-permute-start.2
  10.5 2.6 collective-permute-start
  13.2 1.2 collective-permute-start.6
  14.4 1.8 select_reduce_fusion.4
  16.2 0.5 bitcast_reduce_fusion.4
  18.2 0.1 reduce_sum.136
  18.2 1.2 collective-permute-start.1
  19.5 0.3 collective-permute-start.5
  19.9 1.1 collective-permute-start.7
  21.0 46.7 %collective-permute-done.7 = bf16[2,1030,128]{2,0,1:T(2,128)(2,1)S(1)} collective-permute-done((bf16[2,1030,128]{2,0,1:T(2,128)(2,1)S(1)}, bf16[2,1030,128]{2,0,1:T(2,128)(2,1)S(1)}, u32[]{:S(2)}, u32[]{:S(2)}) %collective-permute-start.7) | collective-permute-done | bytes 527392 | tf_op jit(solution)/shard_map/ppermute | solution.py:19
  67.7 0.8 select_reduce_fusion
  68.5 0.5 bitcast_reduce_fusion
  69.1 0.7 copy-done.2
  69.8 0.8 select_reduce_fusion.1
  70.7 0.5 bitcast_reduce_fusion.1
  71.2 1.0 copy-done.10
  72.2 1.7 select_reduce_fusion.3
  74.0 0.1 reduce_sum.148
  74.2 0.1 reduce_sum.145
  74.3 1.8 bitcast_reduce_fusion.3
  76.2 0.1 reduce_sum.139
  76.3 0.8 select_reduce_fusion.2
  77.1 1.3 copy-done.3
  78.5 0.5 bitcast_reduce_fusion.2
  79.1 0.1 reduce_sum.142
  79.2 0.1 divide_multiply_fusion
  79.3 0.6 fusion.43
  79.9 0.6 fusion.39
  81.8 0.6 fusion.41
  84.4 78.0 %psum.7 = f32[]{:T(128)} all-reduce(f32[]{:T(128)S(6)} %add.226), channel_id=1, replica_groups=mesh['dp'=256] {'dp'}, use_global_device_ids=true, to_apply=%region_20.21 | all-reduce | flops 1 | bytes 8 | tf_op jit(solution)/shard_map/psum | solution.py:78
  162.4 0.1 mul.230
  162.5 1.9 fusion.1
  164.4 0.4 fusion.47
  164.8 4.1 %copy.32 = f32[2,1030,128]{2,0,1:T(2,128)} copy(f32[2,1030,128]{2,1,0:T(8,128)S(1)} %fusion.47) | data formatting | bytes 2109440 | tf_op jit(solution)/shard_map/dot_general | solution.py:47
  169.0 0.1 mul.215
  169.0 1.9 fusion.7
  171.0 0.1 mul.220
  171.0 1.9 fusion.5
  172.9 0.4 fusion.45
  173.3 4.1 %copy.28 = f32[2,1030,128]{2,0,1:T(2,128)} copy(f32[2,1030,128]{2,1,0:T(8,128)S(1)} %fusion.45) | data formatting | bytes 2109440 | tf_op jit(solution)/shard_map/dot_general | solution.py:47
  177.5 0.1 mul.225
  177.6 1.9 fusion.3
  179.5 0.4 fusion.46
  179.9 4.1 %copy.30 = f32[2,1030,128]{2,0,1:T(2,128)} copy(f32[2,1030,128]{2,1,0:T(8,128)S(1)} %fusion.46) | data formatting | bytes 2109440 | tf_op jit(solution)/shard_map/dot_general | solution.py:47
  184.2 0.6 fusion.9
  184.8 0.4 fusion.44
  185.3 3.3 %copy.26 = f32[2,1030,128]{2,0,1:T(2,128)S(1)} copy(f32[2,1030,128]{2,1,0:T(8,128)S(1)} %fusion.44) | data formatting | bytes 2109440 | tf_op jit(solution)/shard_map/dot_general | solution.py:47
  188.6 1.3 collective-permute-start.8
  189.9 3.3 %collective-permute-start.10 = (f32[2,1030,128]{2,0,1:T(2,128)S(1)}, f32[2,1030,128]{2,0,1:T(2,128)S(1)}, u32[]{:S(2)}, u32[]{:S(2)}) collective-permute-start(f32[2,1030,128]{2,0,1:T(2,128)S(1)} %copy-done.14), channel_id=1, source_target_pairs={{0,32},{32,0},{1,33},{33,1},{2,34},{34,2},{3,35},{35,3},{4,36},{36... | collective-permute-start | bytes 3164168 | tf_op jit(solution)/shard_map/ppermute | solution.py:19
  193.2 0.1 collective-permute-start.11
  193.3 0.5 convolution_bitcast_fusion.4
  193.9 0.5 convolution_bitcast_fusion
  194.4 0.5 convolution_bitcast_fusion.2
  195.0 0.1 copy-done.9
  195.1 0.1 copy-done.20
  195.2 0.5 convolution_bitcast_fusion.1
  195.8 1.2 fusion.13
  197.0 17.1 %collective-permute-done.8 = f32[2,1030,128]{2,0,1:T(2,128)S(1)} collective-permute-done((f32[2,1030,128]{2,0,1:T(2,128)S(1)}, f32[2,1030,128]{2,0,1:T(2,128)S(1)}, u32[]{:S(2)}, u32[]{:S(2)}) %collective-permute-start.8) | collective-permute-done | bytes 1054752 | tf_op jit(solution)/shard_map/ppermute | solution.py:19
  214.1 26.6 %collective-permute-done.10 = f32[2,1030,128]{2,0,1:T(2,128)S(1)} collective-permute-done((f32[2,1030,128]{2,0,1:T(2,128)S(1)}, f32[2,1030,128]{2,0,1:T(2,128)S(1)}, u32[]{:S(2)}, u32[]{:S(2)}) %collective-permute-start.10) | collective-permute-done | bytes 1054752 | tf_op jit(solution)/shard_map/ppermute | solution.py:19
  240.7 45.6 %collective-permute-done.11 = f32[2,1030,128]{2,0,1:T(2,128)S(1)} collective-permute-done((f32[2,1030,128]{2,0,1:T(2,128)S(1)}, f32[2,1030,128]{2,0,1:T(2,128)S(1)}, u32[]{:S(2)}, u32[]{:S(2)}) %collective-permute-start.11) | collective-permute-done | bytes 1054752 | tf_op jit(solution)/shard_map/ppermute | solution.py:19
  286.3 0.5 copy_add_fusion
  286.9 4.1 %copy.34 = f32[2,1030,128]{2,0,1:T(2,128)} copy(f32[2,1030,128]{2,1,0:T(8,128)S(1)} %copy_add_fusion) | data formatting | bytes 2109440
  (78 shorter events, 1.0 us)
Async XLA Ops:
  0.6 13.8 %copy-start = (bf16[8,32,128]{2,1,0:T(8,128)(2,1)S(1)}, bf16[8,32,128]{2,1,0:T(8,128)(2,1)}, u32[]{:S(2)}) copy-start(bf16[8,32,128]{2,1,0:T(8,128)(2,1)} %param.6) | copy-start | bytes 196612
  1.4 16.8 %collective-permute-start.4 = (bf16[2,1030]{1,0:T(2,128)(2,1)S(1)}, bf16[2,1030]{1,0:T(2,128)(2,1)S(1)}, u32[]{:S(2)}, u32[]{:S(2)}) collective-permute-start(bf16[2,1030]{1,0:T(2,128)(2,1)S(1)} %get-tuple-element.27), channel_id=1, source_target_pairs={{0,32},{32,0},{1,33},{33,1},{2,34},{34,2},{3,35},{35,3},{4,36},{36... | collective-permute-start | bytes 12368 | tf_op jit(solution)/shard_map/ppermute | solution.py:19
  9.2 10.2 %collective-permute-start.2 = (bf16[2,1030]{1,0:T(2,128)(2,1)S(1)}, bf16[2,1030]{1,0:T(2,128)(2,1)S(1)}, u32[]{:S(2)}, u32[]{:S(2)}) collective-permute-start(bf16[2,1030]{1,0:T(2,128)(2,1)S(1)} %get-tuple-element.27), channel_id=1, source_target_pairs={{0,64},{64,0},{1,65},{65,1},{2,66},{66,2},{3,67},{67,3},{4,68},{68... | collective-permute-start | bytes 12368 | tf_op jit(solution)/shard_map/ppermute | solution.py:19
  10.5 9.3 %collective-permute-start = (bf16[2,1030]{1,0:T(2,128)(2,1)S(1)}, bf16[2,1030]{1,0:T(2,128)(2,1)S(1)}, u32[]{:S(2)}, u32[]{:S(2)}) collective-permute-start(bf16[2,1030]{1,0:T(2,128)(2,1)S(1)} %get-tuple-element.27), channel_id=1, source_target_pairs={{0,128},{128,0},{1,129},{129,1},{2,130},{130,2},{3,131},{131,3},{4... | collective-permute-start | bytes 12368 | tf_op jit(solution)/shard_map/ppermute | solution.py:19
  13.2 7.8 %collective-permute-start.6 = (bf16[2,1030]{1,0:T(2,128)(2,1)S(1)}, bf16[2,1030]{1,0:T(2,128)(2,1)S(1)}, u32[]{:S(2)}, u32[]{:S(2)}) collective-permute-start(bf16[2,1030]{1,0:T(2,128)(2,1)S(1)} %get-tuple-element.27), channel_id=1, source_target_pairs={{0,16},{16,0},{1,17},{17,1},{2,18},{18,2},{3,19},{19,3},{4,20},{20... | collective-permute-start | bytes 12368 | tf_op jit(solution)/shard_map/ppermute | solution.py:19
  14.4 61.9 %collective-permute-start.3 = (bf16[2,1030,128]{2,0,1:T(2,128)(2,1)}, bf16[2,1030,128]{2,0,1:T(2,128)(2,1)S(1)}, u32[]{:S(2)}, u32[]{:S(2)}) collective-permute-start(bf16[2,1030,128]{2,0,1:T(2,128)(2,1)} %param.7), channel_id=1, source_target_pairs={{0,64},{64,0},{1,65},{65,1},{2,66},{66,2},{3,67},{67,3},{4,68},{68... | collective-permute-start | bytes 1582088 | tf_op jit(solution)/shard_map/ppermute | solution.py:19
  14.4 3.9 %copy-start.15 = (bf16[2,1030,128]{2,0,1:T(2,128)(2,1)S(1)}, bf16[2,1030,128]{2,0,1:T(2,128)(2,1)}, u32[]{:S(2)}) copy-start(bf16[2,1030,128]{2,0,1:T(2,128)(2,1)} %param.7) | copy-start | bytes 1582084
  18.2 53.0 %collective-permute-start.1 = (bf16[2,1030,128]{2,0,1:T(2,128)(2,1)S(1)}, bf16[2,1030,128]{2,0,1:T(2,128)(2,1)S(1)}, u32[]{:S(2)}, u32[]{:S(2)}) collective-permute-start(bf16[2,1030,128]{2,0,1:T(2,128)(2,1)S(1)} %copy-done.15), channel_id=1, source_target_pairs={{0,128},{128,0},{1,129},{129,1},{2,130},{130,2},{3,131},{131,3},{4... | collective-permute-start | bytes 1582088 | tf_op jit(solution)/shard_map/ppermute | solution.py:19
  19.5 50.4 %collective-permute-start.5 = (bf16[2,1030,128]{2,0,1:T(2,128)(2,1)S(1)}, bf16[2,1030,128]{2,0,1:T(2,128)(2,1)S(1)}, u32[]{:S(2)}, u32[]{:S(2)}) collective-permute-start(bf16[2,1030,128]{2,0,1:T(2,128)(2,1)S(1)} %copy-done.15), channel_id=1, source_target_pairs={{0,32},{32,0},{1,33},{33,1},{2,34},{34,2},{3,35},{35,3},{4,36},{36... | collective-permute-start | bytes 1582088 | tf_op jit(solution)/shard_map/ppermute | solution.py:19
  19.9 47.9 %collective-permute-start.7 = (bf16[2,1030,128]{2,0,1:T(2,128)(2,1)S(1)}, bf16[2,1030,128]{2,0,1:T(2,128)(2,1)S(1)}, u32[]{:S(2)}, u32[]{:S(2)}) collective-permute-start(bf16[2,1030,128]{2,0,1:T(2,128)(2,1)S(1)} %copy-done.15), channel_id=1, source_target_pairs={{0,16},{16,0},{1,17},{17,1},{2,18},{18,2},{3,19},{19,3},{4,20},{20... | collective-permute-start | bytes 1582088 | tf_op jit(solution)/shard_map/ppermute | solution.py:19
  67.7 1.3 copy-start.21
  68.5 1.3 copy-start.2
  69.8 1.3 copy-start.19
  70.7 3.3 %copy-start.1 = (f32[2,1030,256]{2,1,0:T(8,128)}, f32[2,1030,256]{2,1,0:T(8,128)S(1)}, u32[]{:S(2)}) copy-start(f32[2,1030,256]{2,1,0:T(8,128)S(1)} %get-tuple-element.36) | copy-start | bytes 6328324
  71.2 1.0 copy-start.10
  76.3 2.9 copy-start.23
  76.3 2.7 copy-start.17
  77.1 1.3 copy-start.3
  164.3 4.5 %copy-start.4 = (bf16[2,256,1030]{1,2,0:T(8,128)(2,1)}, bf16[2,256,1030]{1,2,0:T(8,128)(2,1)S(1)}, u32[]{:S(2)}) copy-start(bf16[2,256,1030]{1,2,0:T(8,128)(2,1)S(1)} %fusion.1) | copy-start | bytes 3164164
  172.9 4.6 %copy-start.6 = (bf16[2,256,1030]{1,2,0:T(8,128)(2,1)}, bf16[2,256,1030]{1,2,0:T(8,128)(2,1)S(1)}, u32[]{:S(2)}) copy-start(bf16[2,256,1030]{1,2,0:T(8,128)(2,1)S(1)} %fusion.5) | copy-start | bytes 3164164
  179.5 4.5 %copy-start.8 = (bf16[2,256,1030]{1,2,0:T(8,128)(2,1)}, bf16[2,256,1030]{1,2,0:T(8,128)(2,1)S(1)}, u32[]{:S(2)}) copy-start(bf16[2,256,1030]{1,2,0:T(8,128)(2,1)S(1)} %fusion.3) | copy-start | bytes 3164164
  184.8 5.1 %copy-start.14 = (f32[2,1030,128]{2,0,1:T(2,128)S(1)}, f32[2,1030,128]{2,0,1:T(2,128)}, u32[]{:S(2)}) copy-start(f32[2,1030,128]{2,0,1:T(2,128)} %copy.30) | copy-start | bytes 3164164
  184.8 8.4 %copy-start.13 = (f32[2,1030,128]{2,0,1:T(2,128)S(1)}, f32[2,1030,128]{2,0,1:T(2,128)}, u32[]{:S(2)}) copy-start(f32[2,1030,128]{2,0,1:T(2,128)} %copy.28) | copy-start | bytes 3164164
  184.8 8.4 %copy-start.12 = (f32[2,1030,128]{2,0,1:T(2,128)S(1)}, f32[2,1030,128]{2,0,1:T(2,128)}, u32[]{:S(2)}) copy-start(f32[2,1030,128]{2,0,1:T(2,128)} %copy.32) | copy-start | bytes 3164164
  184.8 8.5 %copy-start.16 = (bf16[2,1030,128]{2,0,1:T(2,128)(2,1)S(1)}, bf16[2,1030,128]{2,0,1:T(2,128)(2,1)}, u32[]{:S(2)}) copy-start(bf16[2,1030,128]{2,0,1:T(2,128)(2,1)} %param.7) | copy-start | bytes 1582084
  185.3 8.6 %copy-start.5 = (bf16[2,256,1030]{1,2,0:T(8,128)(2,1)S(1)}, bf16[2,256,1030]{1,2,0:T(8,128)(2,1)}, u32[]{:S(2)}) copy-start(bf16[2,256,1030]{1,2,0:T(8,128)(2,1)} %copy-done.4) | copy-start | bytes 3164164
  185.3 8.6 %copy-start.22 = (bf16[2,1030,128]{2,0,1:T(2,128)(2,1)S(1)}, bf16[2,1030,128]{2,0,1:T(2,128)(2,1)}, u32[]{:S(2)}) copy-start(bf16[2,1030,128]{2,0,1:T(2,128)(2,1)} %copy-done.21) | copy-start | bytes 1582084
  188.6 5.8 %copy-start.7 = (bf16[2,256,1030]{1,2,0:T(8,128)(2,1)S(1)}, bf16[2,256,1030]{1,2,0:T(8,128)(2,1)}, u32[]{:S(2)}) copy-start(bf16[2,256,1030]{1,2,0:T(8,128)(2,1)} %copy-done.6) | copy-start | bytes 3164164
  188.6 5.8 %copy-start.18 = (bf16[2,1030,128]{2,0,1:T(2,128)(2,1)S(1)}, bf16[2,1030,128]{2,0,1:T(2,128)(2,1)}, u32[]{:S(2)}) copy-start(bf16[2,1030,128]{2,0,1:T(2,128)(2,1)} %copy-done.17) | copy-start | bytes 1582084
  188.6 25.5 %collective-permute-start.8 = (f32[2,1030,128]{2,0,1:T(2,128)S(1)}, f32[2,1030,128]{2,0,1:T(2,128)S(1)}, u32[]{:S(2)}, u32[]{:S(2)}) collective-permute-start(f32[2,1030,128]{2,0,1:T(2,128)S(1)} %copy.26), channel_id=1, source_target_pairs={{0,128},{128,0},{1,129},{129,1},{2,130},{130,2},{3,131},{131,3},{4... | collective-permute-start | bytes 3164168 | tf_op jit(solution)/shard_map/ppermute | solution.py:19
  189.9 50.8 %collective-permute-start.10 = (f32[2,1030,128]{2,0,1:T(2,128)S(1)}, f32[2,1030,128]{2,0,1:T(2,128)S(1)}, u32[]{:S(2)}, u32[]{:S(2)}) collective-permute-start(f32[2,1030,128]{2,0,1:T(2,128)S(1)} %copy-done.14), channel_id=1, source_target_pairs={{0,32},{32,0},{1,33},{33,1},{2,34},{34,2},{3,35},{35,3},{4,36},{36... | collective-permute-start | bytes 3164168 | tf_op jit(solution)/shard_map/ppermute | solution.py:19
  193.2 47.5 %collective-permute-start.9 = (f32[2,1030,128]{2,0,1:T(2,128)S(1)}, f32[2,1030,128]{2,0,1:T(2,128)S(1)}, u32[]{:S(2)}, u32[]{:S(2)}) collective-permute-start(f32[2,1030,128]{2,0,1:T(2,128)S(1)} %copy-done.13), channel_id=1, source_target_pairs={{0,64},{64,0},{1,65},{65,1},{2,66},{66,2},{3,67},{67,3},{4,68},{68... | collective-permute-start | bytes 3164168 | tf_op jit(solution)/shard_map/ppermute | solution.py:19
  193.2 93.1 %collective-permute-start.11 = (f32[2,1030,128]{2,0,1:T(2,128)S(1)}, f32[2,1030,128]{2,0,1:T(2,128)S(1)}, u32[]{:S(2)}, u32[]{:S(2)}) collective-permute-start(f32[2,1030,128]{2,0,1:T(2,128)S(1)} %copy-done.12), channel_id=1, source_target_pairs={{0,16},{16,0},{1,17},{17,1},{2,18},{18,2},{3,19},{19,3},{4,20},{20... | collective-permute-start | bytes 3164168 | tf_op jit(solution)/shard_map/ppermute | solution.py:19
  193.9 1.2 copy-start.9
  193.9 1.4 copy-start.20
  194.4 1.3 copy-start.11
where the time goes:
time: 291 us
  waiting for transfers between devices  136 us (47%)
  blocking collectives  78 us (27%)
  local copies, waits for them, and re-layouts  24.2 us (8%)
  starting transfers between devices  20.3 us (7%)
  other arithmetic  15.2 us (5%)
  matrix products  11.5 us (4%)
  between operations  5.71 us (2%)
    ppermute x12, waiting for transfers between devices, partner_2(): return lax.ppermute(block, axis, route)  136 us
    psum x1, blocking collectives, per_device(): summed_loss = lax.psum(loss_sum, 'dp')  78 us
    ppermute x12, starting transfers between devices, partner_2(): return lax.ppermute(block, axis, route)  20.3 us
    dot_general x4, local copies, waits for them, and re-layouts, block_terms(): lax.dot_general(coefficient, flat_query, (((1,), (0,)), ((), ())), prefer...  15.6 us
    convert_element_type x5, other arithmetic, block_terms(): (weights * jnp.repeat(slopes, q_tok, axis=1)[:, :, None]).astype(jnp.bflo...  8.02 us
    unnamed x49, local copies, waits for them, and re-layouts  7.51 us
    dot_general x5, matrix products, block_terms(): lax.dot_general(page_block, flat_query, (((2,), (1,)), ((), ())), preferr...  5.97 us
  transfers between devices with their start and end apart: 12, of which 4 were waited for; matrix products, arithmetic and copies ran while one was open for 4% of the time, Pallas kernels for 0%

commit v1 on v0

v1 whole, which is shorter than its diff:
```python
import jax
import jax.numpy as jnp
from jax import lax
from jax.experimental import pallas as pl
from jax.experimental.pallas import tpu as pltpu
from jax.sharding import PartitionSpec as P

EMB = 128
QT = 32
TAU = 0.1
EXP2_SCALE = 1.4426950408889634 / TAU
MIN_COUNT = 700
MESH = pl.DeviceIdType.MESH


def kernel(
    n_dev, q_rows, p_rows,
    q_hbm, p_hbm, counts, labels, scale, bias,
    loss_out, gq_out, gp_out,
    qbuf, pg, pgt, xs, gown, gsend, grecv, ones, lvec, lsend, l1, l2,
    local_sem, q_send, q_recv, g_send, g_recv, l_send, l_recv,
):
    me = lax.axis_index("dp")
    n_bits = n_dev.bit_length() - 1
    flip = [(1 << b) - 2 * (1 << b) * ((me // (1 << b)) % 2) for b in range(n_bits)]
    low_bits = n_bits - 4

    def peer(offset):
        out = me
        for b in range(n_bits):
            if offset >> b & 1:
                out = out + flip[b]
        return out

    group_a = [d << low_bits for d in range(1, 16)]
    group_b = list(range(1, 1 << low_bits))
    bits = [n_bits - 2, n_bits - 4, n_bits - 1, n_bits - 3]
    p_pad = pg.shape[0]

    barrier = pltpu.get_barrier_semaphore()
    for d in group_a + group_b:
        pl.semaphore_signal(barrier, inc=1, device_id=(peer(d),), device_id_type=MESH)

    get_q = pltpu.make_async_copy(q_hbm, qbuf.at[0, pl.ds(0, q_rows)], local_sem.at[0])
    get_q.start()
    pg[pl.ds(p_pad - 16, 16), :] = jnp.zeros((16, EMB), jnp.bfloat16)
    get_p = pltpu.make_async_copy(p_hbm.reshape(p_rows, EMB), pg.at[pl.ds(0, p_rows)], local_sem.at[1])
    get_p.start()

    row = lax.broadcasted_iota(jnp.int32, (16, EMB), 0)
    lane = lax.broadcasted_iota(jnp.int32, (16, EMB), 1)
    which = (row & 1) * (EMB // QT) + lane // QT
    label = jnp.zeros((16, EMB), jnp.int32)
    for q in range(q_rows // QT):
        label = jnp.where(which == q, labels[q], label)
    tail = jnp.where(row < 2, label >> 1, label & 1)
    qbuf[0, pl.ds(q_rows, 16), :] = tail.astype(jnp.float32).astype(jnp.bfloat16)

    get_q.wait()
    pl.semaphore_wait(barrier, len(group_a) + len(group_b))

    def q_copy(slot):
        return pltpu.make_async_remote_copy(
            qbuf.at[0], qbuf.at[slot], q_send.at[slot], q_recv.at[slot],
            device_id=(peer(1 << bits[slot - 1]),), device_id_type=MESH,
        )

    q_copies = {slot: q_copy(slot) for slot in (4, 2, 3, 1)}
    for copy in q_copies.values():
        copy.start()

    group_row = lax.broadcasted_iota(jnp.int32, (q_rows, q_rows), 0) // QT
    group_col = lax.broadcasted_iota(jnp.int32, (q_rows, q_rows), 1) // QT
    ones[...] = jnp.where(group_row == group_col, 1.0, 0.0).astype(jnp.bfloat16)
    gp2 = gp_out.reshape(p_rows, EMB)
    main_rows = p_rows // 16 * 16
    sub = lax.broadcasted_iota(jnp.int32, (8, q_rows), 0)
    parity = sub & 1
    limit = 2 * jnp.where(parity == 0, counts[0], counts[1]) - sub
    scale_v = scale[0]
    bias_v = bias[0]
    lvec[...] = jnp.zeros_like(lvec)

    chunk = p_pad // 3
    get_p.wait()
    for c in range(3):
        pgt[c] = pg[pl.ds(c * chunk, chunk), :].astype(jnp.float32).T.astype(jnp.bfloat16)

    def all_rows(vec, op):
        vec = op(vec, pltpu.roll(vec, 2, 0))
        return op(vec, pltpu.roll(vec, 4, 0))

    def forward(k):
        q = qbuf[k, pl.ds(0, q_rows), :]
        top = jnp.full((8, q_rows), -jnp.inf, jnp.float32)
        for c in range(3):
            x = lax.dot_general(
                pg[pl.ds(c * chunk, chunk), :], q, (((1,), (1,)), ((), ())), preferred_element_type=jnp.float32
            ).reshape(chunk // 8, 8, q_rows)
            if (c + 1) * chunk > 2 * MIN_COUNT:
                start = c * chunk + 8 * lax.broadcasted_iota(jnp.int32, x.shape, 0)
                x = jnp.where(limit[None] > start, x, -jnp.inf)
            xs[c] = x
            top = jnp.maximum(top, jnp.max(x, axis=0))
        top = all_rows(top, jnp.maximum)
        total = jnp.zeros((8, q_rows), jnp.float32)
        for c in range(3):
            e = jnp.exp2((xs[c] - top[None]) * EXP2_SCALE)
            xs[c] = e
            total = total + jnp.sum(e, axis=0)
        total = all_rows(total, jnp.add)
        soft = top + TAU * jnp.log(total)
        hi = soft.astype(jnp.bfloat16).astype(jnp.float32)
        rest = soft - hi
        mid = rest.astype(jnp.bfloat16).astype(jnp.float32)
        parts = jnp.concatenate([hi, mid, rest - mid, jnp.zeros_like(hi)], axis=0).astype(jnp.bfloat16)
        sums = jnp.dot(parts, ones[...], preferred_element_type=jnp.float32)
        score = sums[0:8] + sums[8:16] + sums[16:24]
        logit = scale_v * score + bias_v
        tags = qbuf[k, pl.ds(q_rows, 16), :].astype(jnp.float32)
        block = jnp.concatenate([tags[0:1], tags[1:2]], axis=1)
        page = jnp.concatenate([tags[2:3], tags[3:4]], axis=1)
        positive = (block == me.astype(jnp.float32)) & (page == parity.astype(jnp.float32))
        sign = jnp.where(positive, 1.0, -1.0)
        t = -sign * logit
        decay = jnp.exp(-jnp.abs(t))
        lvec[...] += jnp.maximum(t, 0.0) + jnp.log1p(decay)
        slope = -sign * scale_v * jnp.where(t >= 0, 1.0, decay) / (1.0 + decay)
        return slope / total

    def backward(k, factor):
        q = qbuf[k, pl.ds(0, q_rows), :]
        grad_q = jnp.zeros((EMB, q_rows), jnp.float32)
        for c in range(3):
            coef = (xs[c] * factor[None]).reshape(chunk, q_rows).astype(jnp.bfloat16)
            grad_q = grad_q + jnp.dot(pgt[c], coef, preferred_element_type=jnp.float32)
            part = jnp.dot(coef, q, preferred_element_type=jnp.float32)
            rows = min(chunk, p_rows - c * chunk)
            here = pl.ds(c * chunk, rows)

            @pl.when(k == 0)
            def _():
                gp2[here, :] = part[:rows]

            @pl.when(k > 0)
            def _():
                gp2[here, :] += part[:rows]
        return grad_q

    def l_copy(stage, slot, offset):
        return pltpu.make_async_remote_copy(
            lsend.at[stage], (l1, l2)[stage].at[slot], l_send.at[stage], l_recv.at[stage],
            device_id=(peer(offset),), device_id_type=MESH,
        )

    def l_wait(stage, group, sem):
        buf = (l1, l2)[stage].at[pl.ds(1, len(group))]
        pltpu.make_async_copy(buf, buf, sem.at[stage]).wait()

    def tree(v):
        while v.shape[0] > 1:
            half = v.shape[0] // 2
            v = v[:half] + v[half:]
        return v[0]

    def g_copy(k):
        target = me
        for slot in range(1, 5):
            target = target + jnp.where(k == slot, flip[bits[slot - 1]], 0)
        return pltpu.make_async_remote_copy(
            gsend.at[k], grecv.at[k], g_send.at[k], g_recv.at[k], device_id=(target,), device_id_type=MESH,
        )

    def step(k, _):
        @pl.when(k > 0)
        def _():
            pltpu.make_async_copy(qbuf.at[k], qbuf.at[k], q_recv.at[k]).wait()

        factor = forward(k)

        @pl.when(k == 4)
        def _():
            v = jnp.sum(lvec[...], axis=0, keepdims=True)
            v = v[:, :EMB] + v[:, EMB:]
            lsend[0] = v
            l1[0] = v
            for slot, d in enumerate(group_a, 1):
                l_copy(0, slot, d).start()

        grad_q = backward(k, factor)

        @pl.when(k == 0)
        def _():
            gown[...] = grad_q

        @pl.when(k > 0)
        def _():
            gsend[k] = grad_q.astype(jnp.bfloat16)
            g_copy(k).start()

        return 0

    lax.fori_loop(0, 5, step, 0)

    l_wait(0, group_a, l_recv)
    v = tree(l1[...])
    if group_b:
        lsend[1] = v
        l2[0] = v
        for slot, d in enumerate(group_b, 1):
            l_copy(1, slot, d).start()
    grad = gown[...]
    for slot in range(1, 5):
        pltpu.make_async_copy(grecv.at[slot], grecv.at[slot], g_recv.at[slot]).wait()
        grad = grad + grecv[slot].astype(jnp.float32)
    gq_out[...] = grad.T
    if group_b:
        l_wait(1, group_b, l_recv)
        v = tree(l2[...])
    loss_out[0, 0] = jnp.sum(v) * (1.0 / (4 * QT))

    l_wait(0, group_a, l_send)
    if group_b:
        l_wait(1, group_b, l_send)
    for slot in range(1, 5):
        q_copies[slot].wait_send()
        pltpu.make_async_copy(gsend.at[slot], gsend.at[slot], g_send.at[slot]).wait()


def per_device(n_dev, queries, pages, counts, labels, logit_scale, logit_bias):
    n_query, q_tok, emb = queries.shape
    n_page, page_len, _ = pages.shape
    q_rows = n_query * q_tok
    p_rows = n_page * page_len
    p_pad = (p_rows + 47) // 48 * 48
    low = max(1, n_dev // 16)
    vmem = pl.BlockSpec(memory_space=pltpu.VMEM)
    smem = pl.BlockSpec(memory_space=pltpu.SMEM)
    bf16, f32 = jnp.bfloat16, jnp.float32
    loss, grad_q, grad_p = pl.pallas_call(
        lambda *refs: kernel(n_dev, q_rows, p_rows, *refs),
        out_shape=(
            jax.ShapeDtypeStruct((1, 1), f32),
            jax.ShapeDtypeStruct((q_rows, emb), f32),
            jax.ShapeDtypeStruct((page_len, n_page, emb), f32),
        ),
        in_specs=[pl.BlockSpec(memory_space=pltpu.HBM)] * 2 + [smem] * 4,
        out_specs=(smem, vmem, vmem),
        scratch_shapes=[
            pltpu.VMEM((5, q_rows + 16, emb), bf16),
            pltpu.VMEM((p_pad, emb), bf16),
            pltpu.VMEM((3, emb, p_pad // 3), bf16),
            pltpu.VMEM((3, p_pad // 24, 8, q_rows), f32),
            pltpu.VMEM((emb, q_rows), f32),
            pltpu.VMEM((5, emb, q_rows), bf16),
            pltpu.VMEM((5, emb, q_rows), bf16),
            pltpu.VMEM((q_rows, q_rows), bf16),
            pltpu.VMEM((8, q_rows), f32),
            pltpu.VMEM((2, 1, emb), f32),
            pltpu.VMEM((16, 1, emb), f32),
            pltpu.VMEM((low, 1, emb), f32),
            pltpu.SemaphoreType.DMA((2,)),
            pltpu.SemaphoreType.DMA((5,)),
            pltpu.SemaphoreType.DMA((5,)),
            pltpu.SemaphoreType.DMA((5,)),
            pltpu.SemaphoreType.DMA((5,)),
            pltpu.SemaphoreType.DMA((2,)),
            pltpu.SemaphoreType.DMA((2,)),
        ],
        compiler_params=pltpu.CompilerParams(
            collective_id=0, has_side_effects=True, vmem_limit_bytes=32 * 1024 * 1024
        ),
    )(
        queries.reshape(q_rows, emb),
        jnp.transpose(pages, (1, 0, 2)),
        counts,
        labels,
        logit_scale.reshape(1),
        logit_bias.reshape(1),
    )
    return loss.reshape(()), grad_q.reshape(n_query, q_tok, emb), jnp.transpose(grad_p, (1, 0, 2))


def solution(mesh):
    n_dev = mesh.shape["dp"]
    placed = (P("dp", None, None), P("dp", None, None), P("dp"), P("dp"), P(), P())
    return jax.shard_map(
        lambda *args: per_device(n_dev, *args),
        mesh=mesh,
        in_specs=placed,
        out_specs=(P(), P("dp", None, None), P("dp", None, None)),
        check_vma=False,
    )
```

time: 291 us -> 43.4 us (0.15)
  waiting for transfers between devices: 136 us -> 0 us
  blocking collectives: 78 us -> 0 us
  Pallas kernels: 0 us -> 34.6 us
  starting transfers between devices: 20.3 us -> 0 us
  local copies, waits for them, and re-layouts: 24.2 us -> 4.81 us
  other arithmetic: 15.2 us -> 0 us
  matrix products: 11.5 us -> 0 us
    ppermute x12 -> x0, waiting for transfers between devices: 136 us -> none  [partner_2(): return lax.ppermute(block, axis, route)]
    psum x1 -> x0, blocking collectives: 78 us -> none  [per_device(): summed_loss = lax.psum(loss_sum, 'dp')]
    pallas_call x0 -> x1, Pallas kernels: none -> 34.6 us  [per_device(): pl.pallas_call(lambda *refs: kernel(n_dev, q_rows, p_rows, *refs), out_sh...]
    ppermute x12 -> x0, starting transfers between devices: 20.3 us -> none  [partner_2(): return lax.ppermute(block, axis, route)]
    dot_general x4 -> x0, local copies, waits for them, and re-layouts: 15.6 us -> none  [block_terms(): lax.dot_general(coefficient, flat_query, (((1,), (0,)), ((), ())), prefer...]
    dot_general x15 -> x0, matrix products: 11.5 us -> none  [the longest x5 5.97 us: block_terms(): lax.dot_general(page_block, flat_query, (((2,), (1,)), ((), ())), preferr...]
    convert_element_type x6 -> x0, other arithmetic: 8.78 us -> none  [the longest x5 8.02 us: block_terms(): (weights * jnp.repeat(slopes, q_tok, axis=1)[:, :, None]).astype(jnp.bflo...]
    reduce_sum x13 -> x0, other arithmetic: 6.19 us -> none  [the longest x5 3.89 us: block_terms(): row_summation = jnp.sum(power_term, axis=2, keepdims=True)]
  transfers between devices with their start and end apart: 12 -> 0, of which waited for: 4 -> 0; matrix products, arithmetic and copies ran while one was open for 4% -> 0% of each run, Pallas kernels for 0% -> 0%
where the time goes in v1:
time: 43.4 us; the launch traced here: 43.2 us
  Pallas kernels  34.6 us (80%)
  local copies, waits for them, and re-layouts  4.81 us (11%)
  between operations  3.69 us (9%)
    pallas_call x1, Pallas kernels, per_device(): pl.pallas_call(lambda *refs: kernel(n_dev, q_rows, p_rows, *refs), out_sh...  34.6 us
    unnamed x10, local copies, waits for them, and re-layouts  4.81 us

profile of v1, /device:TPU:1, one launch (start us, length us, event | category | flops | bytes accessed | tf_op | source)
XLA Modules:
  0.0 43.2 jit_solution(9735128194570270719)
XLA Ops:
  1.9 0.0 copy-start
  1.9 1.0 %copy-done = bf16[2,1030,128]{2,0,1:T(2,128)(2,1)S(1)} copy-done((bf16[2,1030,128]{2,0,1:T(2,128)(2,1)S(1)}, bf16[2,1030,128]{2,0,1:T(2,128)(2,1)}, u32[]{:S(2)}) %copy-start) | copy-done | bytes 527384
  3.0 0.0 copy-start.1
  3.0 0.8 %copy-done.1 = bf16[8,32,128]{2,1,0:T(8,128)(2,1)S(1)} copy-done((bf16[8,32,128]{2,1,0:T(8,128)(2,1)S(1)}, bf16[8,32,128]{2,1,0:T(8,128)(2,1)}, u32[]{:S(2)}) %copy-start.1) | copy-done | bytes 65560
  3.8 0.0 copy-start.2
  3.8 0.7 %copy-done.2 = s32[2]{0:T(128)S(1)} copy-done((s32[2]{0:T(128)S(1)}, s32[2]{0:T(128)}, u32[]{:S(2)}) %copy-start.2) | copy-done | bytes 32
  4.5 0.0 copy-start.3
  4.5 0.7 %copy-done.3 = s32[8]{0:T(128)S(1)} copy-done((s32[8]{0:T(128)S(1)}, s32[8]{0:T(128)}, u32[]{:S(2)}) %copy-start.3) | copy-done | bytes 56
  5.1 34.6 %shard_map.85 = (f32[1,1]{1,0:T(1,128)}, f32[256,128]{1,0:T(8,128)S(1)}, f32[1030,2,128]{2,1,0:T(2,128)S(1)}) custom-call(bf16[256,128]{1,0:T(8,128)(2,1)S(1)} %bitcast.12, bf16[1030,2,128]{2,1,0:T(2,128)(2,1)S(1)} %bitcast.10, s32[2]{0:T(128)S(1)} %copy-done.2, s32[8]{0:T(128)S(1)} %copy-done.3, f32[1]{0:T(128)} %bitcast.7.refs_4_, f32[1]{0:T(128)} %bitcast.8.refs_5_), custom_call_target="tpu_custom_call" | custom-call | tf_op jit(solution)/shard_map/pallas_call | solution.py:240
  40.4 0.7 %copy.15 = f32[8,32,128]{2,1,0:T(8,128)} copy(f32[8,32,128]{2,1,0:T(8,128)S(1)} %bitcast.11) | data formatting | bytes 262144
  41.1 1.0 %copy.16 = f32[2,1030,128]{2,0,1:T(2,128)} copy(f32[2,1030,128]{2,0,1:T(2,128)S(1)} %bitcast.9) | data formatting | bytes 2109440
Async XLA Ops:
  1.9 1.0 %copy-start = (bf16[2,1030,128]{2,0,1:T(2,128)(2,1)S(1)}, bf16[2,1030,128]{2,0,1:T(2,128)(2,1)}, u32[]{:S(2)}) copy-start(bf16[2,1030,128]{2,0,1:T(2,128)(2,1)} %param.7) | copy-start | bytes 1582084
  3.0 0.8 %copy-start.1 = (bf16[8,32,128]{2,1,0:T(8,128)(2,1)S(1)}, bf16[8,32,128]{2,1,0:T(8,128)(2,1)}, u32[]{:S(2)}) copy-start(bf16[8,32,128]{2,1,0:T(8,128)(2,1)} %param.6) | copy-start | bytes 196612
  3.8 0.7 %copy-start.2 = (s32[2]{0:T(128)S(1)}, s32[2]{0:T(128)}, u32[]{:S(2)}) copy-start(s32[2]{0:T(128)} %refs_2_.1) | copy-start | bytes 28
  4.5 0.7 %copy-start.3 = (s32[8]{0:T(128)S(1)}, s32[8]{0:T(128)}, u32[]{:S(2)}) copy-start(s32[8]{0:T(128)} %refs_3_.1) | copy-start | bytes 100

commit v2 on v1

v2 whole, which is shorter than its diff:
```python
import jax
import jax.numpy as jnp
from jax import lax
from jax.experimental import pallas as pl
from jax.experimental.pallas import tpu as pltpu
from jax.sharding import PartitionSpec as P

EMB = 128
QT = 32
TAU = 0.1
EXP2_SCALE = 1.4426950408889634 / TAU
MIN_COUNT = 700
CHUNKS = 3
MESH = pl.DeviceIdType.MESH


def combos(bits):
    return [sum(1 << b for i, b in enumerate(bits) if s >> i & 1) for s in range(1 << len(bits))]


def far_first(offsets, far):
    return sorted(range(1, len(offsets)), key=lambda s: (-sum(far[b] for b in range(8) if offsets[s] >> b & 1), s))


def kernel(
    n_dev, q_rows, p_rows,
    q_hbm, p_hbm, counts_hbm, labels_hbm, scale_hbm, bias_hbm,
    loss_out, gq_out, gp_out,
    counts, labels, scale, bias,
    qbuf, tags, pg, pgt, xs, tops, totals, factors, gown, gsend, grecv, ones, lsend, l1, l2,
    local_sem, q_send, q_recv, t_send, t_recv, g_send, g_recv, l_send, l_recv,
):
    me = lax.axis_index("dp")
    n_bits = n_dev.bit_length() - 1
    flip = [(1 << b) - 2 * (1 << b) * ((me // (1 << b)) % 2) for b in range(n_bits)]

    def peer(offset):
        out = me
        for b in range(n_bits):
            if offset >> b & 1:
                out = out + flip[b]
        return out

    bits = [n_bits - 2, n_bits - 1, n_bits - 4, n_bits - 3]
    if n_dev == 256:
        groups = [combos([0, 3, 4, 5]), combos([1, 2, 6, 7])]
        far = [0.5, 1, 2, 1, 2, 4, 1, 2]
    else:
        groups = [combos(range(2)), combos(range(2, n_bits))]
        far = [1] * 8
    order = [far_first(g, far) for g in groups]
    p_pad = pg.shape[0]
    chunk = p_pad // CHUNKS

    barrier = pltpu.get_barrier_semaphore()

    def greet(offset):
        pl.semaphore_signal(barrier, inc=1, device_id=(peer(offset),), device_id_type=MESH)

    first = [1 << bits[slot - 1] for slot in (4, 3, 2, 1)]
    others = [g[s] for g, o in zip(groups, order) for s in o if g[s] not in first]
    for d in first:
        greet(d)

    pg[pl.ds(p_pad - 16, 16), :] = jnp.zeros((16, EMB), jnp.bfloat16)
    local = [
        pltpu.make_async_copy(src, dst, local_sem.at[i])
        for i, (src, dst) in enumerate(
            [
                (labels_hbm, labels),
                (q_hbm, qbuf.at[0]),
                (p_hbm.reshape(p_rows, EMB), pg.at[pl.ds(0, p_rows)]),
                (counts_hbm, counts),
                (scale_hbm, scale),
                (bias_hbm, bias),
            ]
        )
    ]
    for copy in local:
        copy.start()
    for d in others:
        greet(d)

    local[0].wait()
    row = lax.broadcasted_iota(jnp.int32, (16, EMB), 0)
    lane = lax.broadcasted_iota(jnp.int32, (16, EMB), 1)
    which = (row & 1) * (EMB // QT) + lane // QT
    label = jnp.zeros((16, EMB), jnp.int32)
    for q in range(q_rows // QT):
        label = jnp.where(which == q, labels[q], label)
    tags[0] = jnp.where(row < 2, label >> 1, label & 1).astype(jnp.float32).astype(jnp.bfloat16)

    pl.semaphore_wait(barrier, len(first) + len(others))

    def q_copy(slot):
        return pltpu.make_async_remote_copy(
            q_hbm, qbuf.at[slot], q_send.at[slot], q_recv.at[slot],
            device_id=(peer(1 << bits[slot - 1]),), device_id_type=MESH,
        )

    def t_copy(slot):
        return pltpu.make_async_remote_copy(
            tags.at[0], tags.at[slot], t_send.at[slot], t_recv.at[slot],
            device_id=(peer(1 << bits[slot - 1]),), device_id_type=MESH,
        )

    for slot in (4, 3, 2, 1):
        q_copy(slot).start()
    for slot in (4, 3, 2, 1):
        t_copy(slot).start()

    group_row = lax.broadcasted_iota(jnp.int32, (q_rows, q_rows), 0) // QT
    group_col = lax.broadcasted_iota(jnp.int32, (q_rows, q_rows), 1) // QT
    ones[...] = jnp.where(group_row == group_col, 1.0, 0.0).astype(jnp.bfloat16)
    gp2 = gp_out.reshape(p_rows, EMB)
    sub = lax.broadcasted_iota(jnp.int32, (8, q_rows), 0)
    parity = sub & 1
    for copy in local[1:]:
        copy.wait()
    limit = 2 * jnp.where(parity == 0, counts[0], counts[1]) - sub

    for c in range(CHUNKS):
        pgt[c] = pg[pl.ds(c * chunk, chunk), :].astype(jnp.float32).T.astype(jnp.bfloat16)

    def all_rows(vec, op):
        vec = op(vec, pltpu.roll(vec, 2, 0))
        return op(vec, pltpu.roll(vec, 4, 0))

    def forward(k, _):
        @pl.when(k > 0)
        def _():
            pltpu.make_async_copy(qbuf.at[k], qbuf.at[k], q_recv.at[k]).wait()

        q = qbuf[k]
        top = jnp.full((8, q_rows), -jnp.inf, jnp.float32)
        for c in range(CHUNKS):
            x = lax.dot_general(
                pg[pl.ds(c * chunk, chunk), :], q, (((1,), (1,)), ((), ())), preferred_element_type=jnp.float32
            ).reshape(chunk // 8, 8, q_rows)
            if (c + 1) * chunk > 2 * MIN_COUNT:
                start = c * chunk + 8 * lax.broadcasted_iota(jnp.int32, x.shape, 0)
                x = jnp.where(limit[None] > start, x, -jnp.inf)
            xs[k, c] = x
            top = jnp.maximum(top, jnp.max(x, axis=0))
        top = all_rows(top, jnp.maximum)
        tops[k] = top
        total = jnp.zeros((8, q_rows), jnp.float32)
        for c in range(CHUNKS):
            e = jnp.exp2((xs[k, c] - top[None]) * EXP2_SCALE)
            xs[k, c] = e
            total = total + jnp.sum(e, axis=0)
        totals[k] = total
        return 0

    lax.fori_loop(0, 5, forward, 0)

    for slot in range(1, 5):
        t_copy(slot).wait_recv()
    parts = []
    total = [all_rows(totals[k], jnp.add) for k in range(5)]
    for k in range(5):
        soft = tops[k] + TAU * jnp.log(total[k])
        hi = soft.astype(jnp.bfloat16).astype(jnp.float32)
        rest = soft - hi
        mid = rest.astype(jnp.bfloat16).astype(jnp.float32)
        parts += [hi, mid, rest - mid]
    parts = jnp.concatenate(parts + [jnp.zeros_like(parts[0])], axis=0).astype(jnp.bfloat16)
    sums = jnp.dot(parts, ones[...], preferred_element_type=jnp.float32).reshape(16, 8, q_rows)
    loss = jnp.zeros((8, q_rows), jnp.float32)
    for k in range(5):
        score = sums[3 * k] + sums[3 * k + 1] + sums[3 * k + 2]
        logit = scale[0] * score + bias[0]
        tag = tags[k].astype(jnp.float32)
        block = jnp.concatenate([tag[0:1], tag[1:2]], axis=1)
        page = jnp.concatenate([tag[2:3], tag[3:4]], axis=1)
        positive = (block == me.astype(jnp.float32)) & (page == parity.astype(jnp.float32))
        sign = jnp.where(positive, 1.0, -1.0)
        t = -sign * logit
        decay = jnp.exp(-jnp.abs(t))
        loss = loss + (jnp.maximum(t, 0.0) + jnp.log1p(decay))
        slope = -sign * scale[0] * jnp.where(t >= 0, 1.0, decay) / (1.0 + decay)
        factors[k] = slope / total[k]

    def l_copy(stage, slot):
        return pltpu.make_async_remote_copy(
            lsend.at[stage], (l1, l2)[stage].at[slot], l_send.at[stage], l_recv.at[stage],
            device_id=(peer(groups[stage][slot]),), device_id_type=MESH,
        )

    def l_wait(stage, sem):
        buf = (l1, l2)[stage].at[pl.ds(1, len(groups[stage]) - 1)]
        pltpu.make_async_copy(buf, buf, sem.at[stage]).wait()

    def l_start(stage, v):
        lsend[stage] = v
        (l1, l2)[stage][0] = v
        for slot in order[stage]:
            l_copy(stage, slot).start()

    def tree(v):
        while v.shape[0] > 1:
            half = v.shape[0] // 2
            v = v[:half] + v[half:]
        return v[0]

    loss = jnp.sum(loss, axis=0, keepdims=True)
    l_start(0, loss[:, :EMB] + loss[:, EMB:])

    def backward(step, _):
        k = 4 - step
        q = qbuf[k]
        factor = factors[k]
        grad_q = jnp.zeros((EMB, q_rows), jnp.float32)
        for c in range(CHUNKS):
            coef = (xs[k, c] * factor[None]).reshape(chunk, q_rows).astype(jnp.bfloat16)
            grad_q = grad_q + jnp.dot(pgt[c], coef, preferred_element_type=jnp.float32)
            part = jnp.dot(coef, q, preferred_element_type=jnp.float32)
            rows = min(chunk, p_rows - c * chunk)
            here = pl.ds(c * chunk, rows)

            @pl.when(step == 0)
            def _():
                gp2[here, :] = part[:rows]

            @pl.when(step > 0)
            def _():
                gp2[here, :] += part[:rows]

        @pl.when(k == 0)
        def _():
            gown[...] = grad_q

        @pl.when(k > 0)
        def _():
            gsend[k] = grad_q.astype(jnp.bfloat16)
            target = me
            for slot in range(1, 5):
                target = target + jnp.where(k == slot, flip[bits[slot - 1]], 0)
            pltpu.make_async_remote_copy(
                gsend.at[k], grecv.at[k], g_send.at[k], g_recv.at[k], device_id=(target,), device_id_type=MESH,
            ).start()

        return 0

    lax.fori_loop(0, 5, backward, 0)

    l_wait(0, l_recv)
    l_start(1, tree(l1[...]))
    grad = gown[...]
    for slot in (1, 2, 3, 4):
        pltpu.make_async_copy(grecv.at[slot], grecv.at[slot], g_recv.at[slot]).wait()
        grad = grad + grecv[slot].astype(jnp.float32)
    gq_out[...] = grad.T
    for slot in range(1, 5):
        q_copy(slot).wait_send()
        t_copy(slot).wait_send()
        pltpu.make_async_copy(gsend.at[slot], gsend.at[slot], g_send.at[slot]).wait()
    l_wait(0, l_send)
    l_wait(1, l_recv)
    loss_out[...] = tree(l2[...])
    l_wait(1, l_send)


def finish(loss, gq, gp, loss_out, gq_out, gp_out, sem):
    copies = [pltpu.make_async_copy(gp, gp_out, sem.at[0]), pltpu.make_async_copy(gq, gq_out, sem.at[1])]
    for copy in copies:
        copy.start()
    loss_out[0, 0] = jnp.sum(loss[...]) * (1.0 / (4 * QT))
    for copy in copies:
        copy.wait()


def per_device(n_dev, queries, pages, counts, labels, logit_scale, logit_bias):
    n_query, q_tok, emb = queries.shape
    n_page, page_len, _ = pages.shape
    q_rows = n_query * q_tok
    p_rows = n_page * page_len
    p_pad = (p_rows + 16 * CHUNKS - 1) // (16 * CHUNKS) * (16 * CHUNKS)
    n2 = 16 if n_dev == 256 else max(2, n_dev // 4)
    vmem = pl.BlockSpec(memory_space=pltpu.VMEM)
    smem = pl.BlockSpec(memory_space=pltpu.SMEM)
    hbm = pl.BlockSpec(memory_space=pltpu.HBM)
    bf16, f32 = jnp.bfloat16, jnp.float32
    dma = pltpu.SemaphoreType.DMA
    gp_shape = jax.ShapeDtypeStruct((page_len, n_page, emb), f32)
    gq_shape = jax.ShapeDtypeStruct((q_rows, emb), f32)
    operands = (
        queries.reshape(q_rows, emb),
        jnp.transpose(pages, (1, 0, 2)),
        counts,
        labels,
        logit_scale.reshape(1),
        logit_bias.reshape(1),
    )
    parts = pl.pallas_call(
        lambda *refs: kernel(n_dev, q_rows, p_rows, *refs),
        out_shape=(jax.ShapeDtypeStruct((1, emb), f32), gq_shape, gp_shape),
        in_specs=[hbm] * 6,
        out_specs=(vmem, vmem, vmem),
        scratch_shapes=[
            pltpu.SMEM(counts.shape, jnp.int32),
            pltpu.SMEM(labels.shape, jnp.int32),
            pltpu.SMEM((1,), f32),
            pltpu.SMEM((1,), f32),
            pltpu.VMEM((5, q_rows, emb), bf16),
            pltpu.VMEM((5, 16, emb), bf16),
            pltpu.VMEM((p_pad, emb), bf16),
            pltpu.VMEM((CHUNKS, emb, p_pad // CHUNKS), bf16),
            pltpu.VMEM((5, CHUNKS, p_pad // (8 * CHUNKS), 8, q_rows), f32),
            pltpu.VMEM((5, 8, q_rows), f32),
            pltpu.VMEM((5, 8, q_rows), f32),
            pltpu.VMEM((5, 8, q_rows), f32),
            pltpu.VMEM((emb, q_rows), f32),
            pltpu.VMEM((5, emb, q_rows), bf16),
            pltpu.VMEM((5, emb, q_rows), bf16),
            pltpu.VMEM((q_rows, q_rows), bf16),
            pltpu.VMEM((2, 1, emb), f32),
            pltpu.VMEM((n_dev // n2, 1, emb), f32),
            pltpu.VMEM((n2, 1, emb), f32),
            dma((6,)),
            dma((5,)),
            dma((5,)),
            dma((5,)),
            dma((5,)),
            dma((5,)),
            dma((5,)),
            dma((2,)),
            dma((2,)),
        ],
        compiler_params=pltpu.CompilerParams(
            collective_id=0, has_side_effects=True, vmem_limit_bytes=40 * 1024 * 1024
        ),
    )(*[pltpu.with_memory_space_constraint(x, pltpu.HBM) for x in operands[:4]], *operands[4:])
    loss, grad_q, grad_p = pl.pallas_call(
        finish,
        out_shape=(jax.ShapeDtypeStruct((1, 1), f32), gq_shape, gp_shape),
        in_specs=[vmem] * 3,
        out_specs=(smem, hbm, hbm),
        scratch_shapes=[dma((2,))],
        compiler_params=pltpu.CompilerParams(vmem_limit_bytes=16 * 1024 * 1024),
    )(*parts)
    return loss.reshape(()), grad_q.reshape(n_query, q_tok, emb), jnp.transpose(grad_p, (1, 0, 2))


def solution(mesh):
    n_dev = mesh.shape["dp"]
    placed = (P("dp", None, None), P("dp", None, None), P("dp"), P("dp"), P(), P())
    return jax.shard_map(
        lambda *args: per_device(n_dev, *args),
        mesh=mesh,
        in_specs=placed,
        out_specs=(P(), P("dp", None, None), P("dp", None, None)),
        check_vma=False,
    )
```

time: 43.4 us -> 34.9 us (0.80)
  local copies, waits for them, and re-layouts: 4.81 us -> 0 us
  between operations: 3.69 us -> 1.93 us
  Pallas kernels: 34.6 us -> 32.9 us
    unnamed x10 -> x0, local copies, waits for them, and re-layouts: 4.81 us -> none
    pallas_call x1, Pallas kernels: 34.6 us -> 31.4 us  [per_device(): pl.pallas_call(lambda *refs: kernel(n_dev, q_rows, p_rows, *refs), out_sh...]
    pallas_call x0 -> x1, Pallas kernels: none -> 1.54 us  [per_device(): pl.pallas_call(finish, out_shape=(jax.ShapeDtypeStruct((1, 1), f32), gq_s...]
where the time goes in v2:
time: 34.9 us; the launch traced here: 34.8 us
  Pallas kernels  32.9 us (94%)
  between operations  1.93 us (6%)
    pallas_call x1, Pallas kernels, per_device(): pl.pallas_call(lambda *refs: kernel(n_dev, q_rows, p_rows, *refs), out_sh...  31.4 us
    pallas_call x1, Pallas kernels, per_device(): pl.pallas_call(finish, out_shape=(jax.ShapeDtypeStruct((1, 1), f32), gq_s...  1.54 us

profile of v2, /device:TPU:1, one launch (start us, length us, event | category | flops | bytes accessed | tf_op | source)
XLA Modules:
  0.0 34.8 jit_solution(18405865993422739083)
XLA Ops:
  1.9 31.4 %shard_map.85 = (f32[1,128]{1,0:T(1,128)S(1)}, f32[256,128]{1,0:T(8,128)S(1)}, f32[1030,2,128]{2,1,0:T(2,128)S(1)}) custom-call(bf16[256,128]{1,0:T(8,128)(2,1)} %bitcast.10, bf16[1030,2,128]{2,1,0:T(2,128)(2,1)} %bitcast.9, s32[2]{0:T(128)} %refs_2_.1, s32[8]{0:T(128)} %refs_3_.1, f32[1]{0:T(128)} %bitcast.7.refs_4_, f32[1]{0:T(128)} %bitcast.8.refs_5_), custom_call_target="tpu_custom_call" | custom-call | tf_op jit(solution)/shard_map/pallas_call | solution.py:295
  33.3 1.5 %shard_map.86 = (f32[1,1]{1,0:T(1,128)}, f32[256,128]{1,0:T(8,128)}, f32[1030,2,128]{2,1,0:T(2,128)}) custom-call(f32[1,128]{1,0:T(1,128)S(1)} %get-tuple-element.9.loss, f32[256,128]{1,0:T(8,128)S(1)} %get-tuple-element.10.gq, f32[1030,2,128]{2,1,0:T(2,128)S(1)} %get-tuple-element.11.gp), custom_call_target="tpu_custom_call" | custom-call | tf_op jit(solution)/shard_map/pallas_call | solution.py:334

commit v3 on v2

--- a/solution.py
+++ b/solution.py
@@ -11,6 +11,7 @@
 EXP2_SCALE = 1.4426950408889634 / TAU
 MIN_COUNT = 700
 CHUNKS = 3
+PIECES = 4
 MESH = pl.DeviceIdType.MESH
 
 
@@ -20,6 +21,11 @@
 
 def far_first(offsets, far):
     return sorted(range(1, len(offsets)), key=lambda s: (-sum(far[b] for b in range(8) if offsets[s] >> b & 1), s))
+
+
+def loss_groups(n_bits):
+    first = [1, 2, 6, 7] if n_bits == 8 else list(range(n_bits // 2))
+    return [combos(first), combos([b for b in range(n_bits) if b not in first])]
 
 
 def kernel(
@@ -27,8 +33,8 @@
     q_hbm, p_hbm, counts_hbm, labels_hbm, scale_hbm, bias_hbm,
     loss_out, gq_out, gp_out,
     counts, labels, scale, bias,
-    qbuf, tags, pg, pgt, xs, tops, totals, factors, gown, gsend, grecv, ones, lsend, l1, l2,
-    local_sem, q_send, q_recv, t_send, t_recv, g_send, g_recv, l_send, l_recv,
+    qbuf, pg, pgt, xs, tops, totals, factors, gown, gsend, grecv, ones, lsend, l1, l2,
+    local_sem, q_send, q_recv, g_send, g_recv, l_send, l_recv,
 ):
     me = lax.axis_index("dp")
     n_bits = n_dev.bit_length() - 1
@@ -41,13 +47,10 @@
                 out = out + flip[b]
         return out
 
-    bits = [n_bits - 2, n_bits - 1, n_bits - 4, n_bits - 3]
-    if n_dev == 256:
-        groups = [combos([0, 3, 4, 5]), combos([1, 2, 6, 7])]
-        far = [0.5, 1, 2, 1, 2, 4, 1, 2]
-    else:
-        groups = [combos(range(2)), combos(range(2, n_bits))]
-        far = [1] * 8
+    bits = [n_bits - 2, n_bits - 1, n_bits - 3, n_bits - 4]
+    groups = loss_groups(n_bits)
+    far = [0.5, 1, 2, 1, 2, 4, 1, 2]
+    lbufs = (l1, l2)
     order = [far_first(g, far) for g in groups]
     p_pad = pg.shape[0]
     chunk = p_pad // CHUNKS
@@ -57,8 +60,9 @@
     def greet(offset):
         pl.semaphore_signal(barrier, inc=1, device_id=(peer(offset),), device_id_type=MESH)
 
-    first = [1 << bits[slot - 1] for slot in (4, 3, 2, 1)]
-    others = [g[s] for g, o in zip(groups, order) for s in o if g[s] not in first]
+    first = [1 << bits[slot - 1] for slot in (3, 4, 2, 1)]
+    others = [groups[i][order[i][n]] for n in range(len(order[0])) for i in (0, 1) if n < len(order[i])]
+    others = [d for d in others if d not in first]
     for d in first:
         greet(d)
 
@@ -68,7 +72,7 @@
         for i, (src, dst) in enumerate(
             [
                 (labels_hbm, labels),
-                (q_hbm, qbuf.at[0]),
+                (q_hbm, qbuf.at[0, pl.ds(0, q_rows)]),
                 (p_hbm.reshape(p_rows, EMB), pg.at[pl.ds(0, p_rows)]),
                 (counts_hbm, counts),
                 (scale_hbm, scale),
@@ -76,10 +80,10 @@
             ]
         )
     ]
+    for d in others:
+        greet(d)
     for copy in local:
         copy.start()
-    for d in others:
-        greet(d)
 
     local[0].wait()
     row = lax.broadcasted_iota(jnp.int32, (16, EMB), 0)
@@ -88,39 +92,33 @@
     label = jnp.zeros((16, EMB), jnp.int32)
     for q in range(q_rows // QT):
         label = jnp.where(which == q, labels[q], label)
-    tags[0] = jnp.where(row < 2, label >> 1, label & 1).astype(jnp.float32).astype(jnp.bfloat16)
-
+    qbuf[0, pl.ds(q_rows, 16), :] = jnp.where(row < 2, label >> 1, label & 1).astype(jnp.float32).astype(jnp.bfloat16)
+
+    local[1].wait()
     pl.semaphore_wait(barrier, len(first) + len(others))
 
     def q_copy(slot):
         return pltpu.make_async_remote_copy(
-            q_hbm, qbuf.at[slot], q_send.at[slot], q_recv.at[slot],
+            qbuf.at[0], qbuf.at[slot], q_send.at[slot], q_recv.at[slot],
             device_id=(peer(1 << bits[slot - 1]),), device_id_type=MESH,
         )
 
-    def t_copy(slot):
-        return pltpu.make_async_remote_copy(
-            tags.at[0], tags.at[slot], t_send.at[slot], t_recv.at[slot],
-            device_id=(peer(1 << bits[slot - 1]),), device_id_type=MESH,
-        )
-
-    for slot in (4, 3, 2, 1):
+    for slot in (3, 4, 2, 1):
         q_copy(slot).start()
-    for slot in (4, 3, 2, 1):
-        t_copy(slot).start()
 
     group_row = lax.broadcasted_iota(jnp.int32, (q_rows, q_rows), 0) // QT
     group_col = lax.broadcasted_iota(jnp.int32, (q_rows, q_rows), 1) // QT
     ones[...] = jnp.where(group_row == group_col, 1.0, 0.0).astype(jnp.bfloat16)
-    gp2 = gp_out.reshape(p_rows, EMB)
     sub = lax.broadcasted_iota(jnp.int32, (8, q_rows), 0)
     parity = sub & 1
-    for copy in local[1:]:
+    for copy in local[2:]:
         copy.wait()
     limit = 2 * jnp.where(parity == 0, counts[0], counts[1]) - sub
 
     for c in range(CHUNKS):
         pgt[c] = pg[pl.ds(c * chunk, chunk), :].astype(jnp.float32).T.astype(jnp.bfloat16)
+
+    gp_out[...] = jnp.zeros_like(gp_out)
 
     def all_rows(vec, op):
         vec = op(vec, pltpu.roll(vec, 2, 0))
@@ -131,7 +129,7 @@
         def _():
             pltpu.make_async_copy(qbuf.at[k], qbuf.at[k], q_recv.at[k]).wait()
 
-        q = qbuf[k]
+        q = qbuf[k, pl.ds(0, q_rows), :]
         top = jnp.full((8, q_rows), -jnp.inf, jnp.float32)
         for c in range(CHUNKS):
             x = lax.dot_general(
@@ -150,12 +148,11 @@
             xs[k, c] = e
             total = total + jnp.sum(e, axis=0)
         totals[k] = total
+
         return 0
 
     lax.fori_loop(0, 5, forward, 0)
 
-    for slot in range(1, 5):
-        t_copy(slot).wait_recv()
     parts = []
     total = [all_rows(totals[k], jnp.add) for k in range(5)]
     for k in range(5):
@@ -170,7 +167,7 @@
     for k in range(5):
         score = sums[3 * k] + sums[3 * k + 1] + sums[3 * k + 2]
         logit = scale[0] * score + bias[0]
-        tag = tags[k].astype(jnp.float32)
+        tag = qbuf[k, pl.ds(q_rows, 16), :].astype(jnp.float32)
         block = jnp.concatenate([tag[0:1], tag[1:2]], axis=1)
         page = jnp.concatenate([tag[2:3], tag[3:4]], axis=1)
         positive = (block == me.astype(jnp.float32)) & (page == parity.astype(jnp.float32))
@@ -183,17 +180,17 @@
 
     def l_copy(stage, slot):
         return pltpu.make_async_remote_copy(
-            lsend.at[stage], (l1, l2)[stage].at[slot], l_send.at[stage], l_recv.at[stage],
+            lsend.at[stage], lbufs[stage].at[slot], l_send.at[stage], l_recv.at[stage],
             device_id=(peer(groups[stage][slot]),), device_id_type=MESH,
         )
 
     def l_wait(stage, sem):
-        buf = (l1, l2)[stage].at[pl.ds(1, len(groups[stage]) - 1)]
+        buf = lbufs[stage].at[pl.ds(1, len(groups[stage]) - 1)]
         pltpu.make_async_copy(buf, buf, sem.at[stage]).wait()
 
     def l_start(stage, v):
         lsend[stage] = v
-        (l1, l2)[stage][0] = v
+        lbufs[stage][0] = v
         for slot in order[stage]:
             l_copy(stage, slot).start()
 
@@ -208,23 +205,16 @@
 
     def backward(step, _):
         k = 4 - step
-        q = qbuf[k]
+        q = qbuf[k, pl.ds(0, q_rows), :]
         factor = factors[k]
         grad_q = jnp.zeros((EMB, q_rows), jnp.float32)
         for c in range(CHUNKS):
             coef = (xs[k, c] * factor[None]).reshape(chunk, q_rows).astype(jnp.bfloat16)
             grad_q = grad_q + jnp.dot(pgt[c], coef, preferred_element_type=jnp.float32)
             part = jnp.dot(coef, q, preferred_element_type=jnp.float32)
-            rows = min(chunk, p_rows - c * chunk)
-            here = pl.ds(c * chunk, rows)
-
-            @pl.when(step == 0)
-            def _():
-                gp2[here, :] = part[:rows]
-
-            @pl.when(step > 0)
-            def _():
-                gp2[here, :] += part[:rows]
+            here = pl.ds(c * chunk, chunk)
+
+            gp_out[here, :] += part
 
         @pl.when(k == 0)
         def _():
@@ -253,7 +243,6 @@
     gq_out[...] = grad.T
     for slot in range(1, 5):
         q_copy(slot).wait_send()
-        t_copy(slot).wait_send()
         pltpu.make_async_copy(gsend.at[slot], gsend.at[slot], g_send.at[slot]).wait()
     l_wait(0, l_send)
     l_wait(1, l_recv)
@@ -262,7 +251,14 @@
 
 
 def finish(loss, gq, gp, loss_out, gq_out, gp_out, sem):
-    copies = [pltpu.make_async_copy(gp, gp_out, sem.at[0]), pltpu.make_async_copy(gq, gq_out, sem.at[1])]
+    n_page, emb = gp_out.shape[1:]
+    rows = gp_out.shape[0] * n_page
+    flat = gp_out.reshape(rows, emb)
+    step = (rows // PIECES + 7) // 8 * 8
+    copies = [pltpu.make_async_copy(gq, gq_out, sem.at[PIECES])]
+    for i in range(PIECES):
+        part = pl.ds(i * step, min(step, rows - i * step))
+        copies.append(pltpu.make_async_copy(gp.at[part], flat.at[part], sem.at[i]))
     for copy in copies:
         copy.start()
     loss_out[0, 0] = jnp.sum(loss[...]) * (1.0 / (4 * QT))
@@ -276,7 +272,7 @@
     q_rows = n_query * q_tok
     p_rows = n_page * page_len
     p_pad = (p_rows + 16 * CHUNKS - 1) // (16 * CHUNKS) * (16 * CHUNKS)
-    n2 = 16 if n_dev == 256 else max(2, n_dev // 4)
+    sizes = [len(g) for g in loss_groups(n_dev.bit_length() - 1)]
     vmem = pl.BlockSpec(memory_space=pltpu.VMEM)
     smem = pl.BlockSpec(memory_space=pltpu.SMEM)
     hbm = pl.BlockSpec(memory_space=pltpu.HBM)
@@ -294,7 +290,7 @@
     )
     parts = pl.pallas_call(
         lambda *refs: kernel(n_dev, q_rows, p_rows, *refs),
-        out_shape=(jax.ShapeDtypeStruct((1, emb), f32), gq_shape, gp_shape),
+        out_shape=(jax.ShapeDtypeStruct((1, emb), f32), gq_shape, jax.ShapeDtypeStruct((p_pad, emb), f32)),
         in_specs=[hbm] * 6,
         out_specs=(vmem, vmem, vmem),
         scratch_shapes=[
@@ -302,8 +298,7 @@
             pltpu.SMEM(labels.shape, jnp.int32),
             pltpu.SMEM((1,), f32),
             pltpu.SMEM((1,), f32),
-            pltpu.VMEM((5, q_rows, emb), bf16),
-            pltpu.VMEM((5, 16, emb), bf16),
+            pltpu.VMEM((5, q_rows + 16, emb), bf16),
             pltpu.VMEM((p_pad, emb), bf16),
             pltpu.VMEM((CHUNKS, emb, p_pad // CHUNKS), bf16),
             pltpu.VMEM((5, CHUNKS, p_pad // (8 * CHUNKS), 8, q_rows), f32),
@@ -315,11 +310,8 @@
             pltpu.VMEM((5, emb, q_rows), bf16),
             pltpu.VMEM((q_rows, q_rows), bf16),
             pltpu.VMEM((2, 1, emb), f32),
-            pltpu.VMEM((n_dev // n2, 1, emb), f32),
-            pltpu.VMEM((n2, 1, emb), f32),
+            *[pltpu.VMEM((n, 1, emb), f32) for n in sizes],
             dma((6,)),
-            dma((5,)),
-            dma((5,)),
             dma((5,)),
             dma((5,)),
             dma((5,)),
@@ -336,7 +328,7 @@
         out_shape=(jax.ShapeDtypeStruct((1, 1), f32), gq_shape, gp_shape),
         in_specs=[vmem] * 3,
         out_specs=(smem, hbm, hbm),
-        scratch_shapes=[dma((2,))],
+        scratch_shapes=[dma((PIECES + 1,))],
         compiler_params=pltpu.CompilerParams(vmem_limit_bytes=16 * 1024 * 1024),
     )(*parts)
     return loss.reshape(()), grad_q.reshape(n_query, q_tok, emb), jnp.transpose(grad_p, (1, 0, 2))

time: 34.9 us -> 32.8 us (0.940)
  Pallas kernels: 32.9 us -> 30.7 us
    pallas_call x1, Pallas kernels: 31.4 us -> 29.1 us  [per_device(): pl.pallas_call(lambda *refs: kernel(n_dev, q_rows, p_rows, *refs), out_sh...]
where the time goes in v3:
time: 32.8 us; the launch traced here: 32.6 us
  Pallas kernels  30.7 us (94%)
  between operations  1.93 us (6%)
    pallas_call x1, Pallas kernels, per_device(): pl.pallas_call(lambda *refs: kernel(n_dev, q_rows, p_rows, *refs), out_sh...  29.1 us
    pallas_call x1, Pallas kernels, per_device(): pl.pallas_call(finish, out_shape=(jax.ShapeDtypeStruct((1, 1), f32), gq_s...  1.56 us

profile of v3, /device:TPU:1, one launch (start us, length us, event | category | flops | bytes accessed | tf_op | source)
XLA Modules:
  0.0 32.6 jit_solution(6847283243102299736)
XLA Ops:
  1.9 29.1 %shard_map.85 = (f32[1,128]{1,0:T(1,128)S(1)}, f32[256,128]{1,0:T(8,128)S(1)}, f32[2064,128]{1,0:T(8,128)S(1)}) custom-call(bf16[256,128]{1,0:T(8,128)(2,1)} %bitcast.10, bf16[1030,2,128]{2,1,0:T(2,128)(2,1)} %bitcast.9, s32[2]{0:T(128)} %refs_2_.1, s32[8]{0:T(128)} %refs_3_.1, f32[1]{0:T(128)} %bitcast.7.refs_4_, f32[1]{0:T(128)} %bitcast.8.refs_5_), custom_call_target="tpu_custom_call" | custom-call | tf_op jit(solution)/shard_map/pallas_call | solution.py:291
  31.1 1.6 %shard_map.86 = (f32[1,1]{1,0:T(1,128)}, f32[256,128]{1,0:T(8,128)}, f32[1030,2,128]{2,1,0:T(2,128)}) custom-call(f32[1,128]{1,0:T(1,128)S(1)} %get-tuple-element.9.loss, f32[256,128]{1,0:T(8,128)S(1)} %get-tuple-element.10.gq, f32[2064,128]{1,0:T(8,128)S(1)} %get-tuple-element.11.gp), custom_call_target="tpu_custom_call" | custom-call | tf_op jit(solution)/shard_map/pallas_call | solution.py:326

commit v4 on v3

--- a/solution.py
+++ b/solution.py
@@ -11,7 +11,6 @@
 EXP2_SCALE = 1.4426950408889634 / TAU
 MIN_COUNT = 700
 CHUNKS = 3
-PIECES = 4
 MESH = pl.DeviceIdType.MESH
 
 
@@ -24,7 +23,7 @@
 
 
 def loss_groups(n_bits):
-    first = [1, 2, 6, 7] if n_bits == 8 else list(range(n_bits // 2))
+    first = [0, 1, 2, 6, 7] if n_bits == 8 else list(range(n_bits // 2))
     return [combos(first), combos([b for b in range(n_bits) if b not in first])]
 
 
@@ -61,7 +60,7 @@
         pl.semaphore_signal(barrier, inc=1, device_id=(peer(offset),), device_id_type=MESH)
 
     first = [1 << bits[slot - 1] for slot in (3, 4, 2, 1)]
-    others = [groups[i][order[i][n]] for n in range(len(order[0])) for i in (0, 1) if n < len(order[i])]
+    others = [groups[i][order[i][n]] for n in range(31) for i in (0, 1) if n < len(order[i])]
     others = [d for d in others if d not in first]
     for d in first:
         greet(d)
@@ -250,18 +249,18 @@
     l_wait(1, l_send)
 
 
-def finish(loss, gq, gp, loss_out, gq_out, gp_out, sem):
+def finish(loss, gq, gp, loss_out, gq_out, gp_out, total, sem):
     n_page, emb = gp_out.shape[1:]
-    rows = gp_out.shape[0] * n_page
-    flat = gp_out.reshape(rows, emb)
-    step = (rows // PIECES + 7) // 8 * 8
-    copies = [pltpu.make_async_copy(gq, gq_out, sem.at[PIECES])]
-    for i in range(PIECES):
-        part = pl.ds(i * step, min(step, rows - i * step))
-        copies.append(pltpu.make_async_copy(gp.at[part], flat.at[part], sem.at[i]))
-    for copy in copies:
-        copy.start()
-    loss_out[0, 0] = jnp.sum(loss[...]) * (1.0 / (4 * QT))
+    flat = gp_out.reshape(gp_out.shape[0] * n_page, emb)
+    copies = [
+        pltpu.make_async_copy(gp.at[pl.ds(0, flat.shape[0])], flat, sem.at[0]),
+        pltpu.make_async_copy(gq, gq_out, sem.at[1]),
+        pltpu.make_async_copy(total, loss_out, sem.at[2]),
+    ]
+    copies[0].start()
+    copies[1].start()
+    total[0, 0] = jnp.sum(loss[...]) * (1.0 / (4 * QT))
+    copies[2].start()
     for copy in copies:
         copy.wait()
 
@@ -274,7 +273,6 @@
     p_pad = (p_rows + 16 * CHUNKS - 1) // (16 * CHUNKS) * (16 * CHUNKS)
     sizes = [len(g) for g in loss_groups(n_dev.bit_length() - 1)]
     vmem = pl.BlockSpec(memory_space=pltpu.VMEM)
-    smem = pl.BlockSpec(memory_space=pltpu.SMEM)
     hbm = pl.BlockSpec(memory_space=pltpu.HBM)
     bf16, f32 = jnp.bfloat16, jnp.float32
     dma = pltpu.SemaphoreType.DMA
@@ -327,8 +325,8 @@
         finish,
         out_shape=(jax.ShapeDtypeStruct((1, 1), f32), gq_shape, gp_shape),
         in_specs=[vmem] * 3,
-        out_specs=(smem, hbm, hbm),
-        scratch_shapes=[dma((PIECES + 1,))],
+        out_specs=(hbm, hbm, hbm),
+        scratch_shapes=[pltpu.SMEM((1, 1), f32), dma((3,))],
         compiler_params=pltpu.CompilerParams(vmem_limit_bytes=16 * 1024 * 1024),
     )(*parts)
     return loss.reshape(()), grad_q.reshape(n_query, q_tok, emb), jnp.transpose(grad_p, (1, 0, 2))

time: 32.8 us -> 31.7 us (0.966)
  Pallas kernels: 30.7 us -> 29.7 us
    pallas_call x1, Pallas kernels: 1.56 us -> 1.04 us  [per_device(): pl.pallas_call(finish, out_shape=(jax.ShapeDtypeStruct((1, 1), f32), gq_s...]
    pallas_call x1, Pallas kernels: 29.1 us -> 28.6 us  [per_device(): pl.pallas_call(lambda *refs: kernel(n_dev, q_rows, p_rows, *refs), out_sh...]
where the time goes in v4:
time: 31.7 us; the launch traced here: 31.6 us
  Pallas kernels  29.7 us (94%)
  between operations  1.93 us (6%)
    pallas_call x1, Pallas kernels, per_device(): pl.pallas_call(lambda *refs: kernel(n_dev, q_rows, p_rows, *refs), out_sh...  28.6 us
    pallas_call x1, Pallas kernels, per_device(): pl.pallas_call(finish, out_shape=(jax.ShapeDtypeStruct((1, 1), f32), gq_s...  1.04 us

profile of v4, /device:TPU:1, one launch (start us, length us, event | category | flops | bytes accessed | tf_op | source)
XLA Modules:
  0.0 31.6 jit_solution(7338767992530444506)
XLA Ops:
  1.9 28.6 %shard_map.85 = (f32[1,128]{1,0:T(1,128)S(1)}, f32[256,128]{1,0:T(8,128)S(1)}, f32[2064,128]{1,0:T(8,128)S(1)}) custom-call(bf16[256,128]{1,0:T(8,128)(2,1)} %bitcast.10, bf16[1030,2,128]{2,1,0:T(2,128)(2,1)} %bitcast.9, s32[2]{0:T(128)} %refs_2_.1, s32[8]{0:T(128)} %refs_3_.1, f32[1]{0:T(128)} %bitcast.7.refs_4_, f32[1]{0:T(128)} %bitcast.8.refs_5_), custom_call_target="tpu_custom_call" | custom-call | tf_op jit(solution)/shard_map/pallas_call | solution.py:289
  30.6 1.0 %shard_map.86 = (f32[1,1]{1,0:T(1,128)}, f32[256,128]{1,0:T(8,128)}, f32[1030,2,128]{2,1,0:T(2,128)}) custom-call(f32[1,128]{1,0:T(1,128)S(1)} %get-tuple-element.9.loss, f32[256,128]{1,0:T(8,128)S(1)} %get-tuple-element.10.gq, f32[2064,128]{1,0:T(8,128)S(1)} %get-tuple-element.11.gp), custom_call_target="tpu_custom_call" | custom-call | tf_op jit(solution)/shard_map/pallas_call | solution.py:324

commit v5 on v4

--- a/solution.py
+++ b/solution.py
@@ -22,9 +22,13 @@
     return sorted(range(1, len(offsets)), key=lambda s: (-sum(far[b] for b in range(8) if offsets[s] >> b & 1), s))
 
 
+def axes(n_bits):
+    return [[0], [1, 2], [3, 4, 5], [6, 7]] if n_bits == 8 else [[0], [1], [2], [3]]
+
+
 def loss_groups(n_bits):
-    first = [0, 1, 2, 6, 7] if n_bits == 8 else list(range(n_bits // 2))
-    return [combos(first), combos([b for b in range(n_bits) if b not in first])]
+    core, x, z, y = axes(n_bits)
+    return [combos(core + x + y), combos(z)]
 
 
 def kernel(
@@ -33,7 +37,7 @@
     loss_out, gq_out, gp_out,
     counts, labels, scale, bias,
     qbuf, pg, pgt, xs, tops, totals, factors, gown, gsend, grecv, ones, lsend, l1, l2,
-    local_sem, q_send, q_recv, g_send, g_recv, l_send, l_recv,
+    local_sem, q_send, q_recv, g_send, g_recv, l_send, l_recv, column_sem, core_sem,
 ):
     me = lax.axis_index("dp")
     n_bits = n_dev.bit_length() - 1
@@ -59,9 +63,9 @@
     def greet(offset):
         pl.semaphore_signal(barrier, inc=1, device_id=(peer(offset),), device_id_type=MESH)
 
+    core, _, _, column = [combos(axis)[1:] for axis in axes(n_bits)]
     first = [1 << bits[slot - 1] for slot in (3, 4, 2, 1)]
-    others = [groups[i][order[i][n]] for n in range(31) for i in (0, 1) if n < len(order[i])]
-    others = [d for d in others if d not in first]
+    others = [d for axis in axes(n_bits) for d in combos(axis)[1:] if d not in first]
     for d in first:
         greet(d)
 
@@ -105,6 +109,12 @@
     for slot in (3, 4, 2, 1):
         q_copy(slot).start()
 
+    def vouch(sem, offsets):
+        for d in offsets:
+            pl.semaphore_signal(sem, inc=1, device_id=(peer(d),), device_id_type=MESH)
+
+    vouch(column_sem, column)
+
     group_row = lax.broadcasted_iota(jnp.int32, (q_rows, q_rows), 0) // QT
     group_col = lax.broadcasted_iota(jnp.int32, (q_rows, q_rows), 1) // QT
     ones[...] = jnp.where(group_row == group_col, 1.0, 0.0).astype(jnp.bfloat16)
@@ -127,6 +137,11 @@
         @pl.when(k > 0)
         def _():
             pltpu.make_async_copy(qbuf.at[k], qbuf.at[k], q_recv.at[k]).wait()
+
+        @pl.when(k == 2)
+        def _():
+            pl.semaphore_wait(column_sem, len(column))
+            vouch(core_sem, core)
 
         q = qbuf[k, pl.ds(0, q_rows), :]
         top = jnp.full((8, q_rows), -jnp.inf, jnp.float32)
@@ -200,6 +215,7 @@
         return v[0]
 
     loss = jnp.sum(loss, axis=0, keepdims=True)
+    pl.semaphore_wait(core_sem, len(core))
     l_start(0, loss[:, :EMB] + loss[:, EMB:])
 
     def backward(step, _):
@@ -316,6 +332,8 @@
             dma((5,)),
             dma((2,)),
             dma((2,)),
+            pltpu.SemaphoreType.REGULAR,
+            pltpu.SemaphoreType.REGULAR,
         ],
         compiler_params=pltpu.CompilerParams(
             collective_id=0, has_side_effects=True, vmem_limit_bytes=40 * 1024 * 1024

time: 31.7 us -> 31.2 us (0.984)
  Pallas kernels: 29.7 us -> 29.1 us
    pallas_call x1, Pallas kernels: 28.6 us -> 28.1 us  [per_device(): pl.pallas_call(lambda *refs: kernel(n_dev, q_rows, p_rows, *refs), out_sh...]
where the time goes in v5:
time: 31.2 us; the launch traced here: 31.1 us
  Pallas kernels  29.1 us (93%)
  between operations  1.93 us (6%)
    pallas_call x1, Pallas kernels, per_device(): pl.pallas_call(lambda *refs: kernel(n_dev, q_rows, p_rows, *refs), out_sh...  28.1 us
    pallas_call x1, Pallas kernels, per_device(): pl.pallas_call(finish, out_shape=(jax.ShapeDtypeStruct((1, 1), f32), gq_s...  1.04 us

profile of v5, /device:TPU:1, one launch (start us, length us, event | category | flops | bytes accessed | tf_op | source)
XLA Modules:
  0.0 31.1 jit_solution(8007472108456665806)
XLA Ops:
  1.9 28.1 %shard_map.85 = (f32[1,128]{1,0:T(1,128)S(1)}, f32[256,128]{1,0:T(8,128)S(1)}, f32[2064,128]{1,0:T(8,128)S(1)}) custom-call(bf16[256,128]{1,0:T(8,128)(2,1)} %bitcast.10, bf16[1030,2,128]{2,1,0:T(2,128)(2,1)} %bitcast.9, s32[2]{0:T(128)} %refs_2_.1, s32[8]{0:T(128)} %refs_3_.1, f32[1]{0:T(128)} %bitcast.7.refs_4_, f32[1]{0:T(128)} %bitcast.8.refs_5_), custom_call_target="tpu_custom_call" | custom-call | tf_op jit(solution)/shard_map/pallas_call | solution.py:305
  30.0 1.0 %shard_map.86 = (f32[1,1]{1,0:T(1,128)}, f32[256,128]{1,0:T(8,128)}, f32[1030,2,128]{2,1,0:T(2,128)}) custom-call(f32[1,128]{1,0:T(1,128)S(1)} %get-tuple-element.9.loss, f32[256,128]{1,0:T(8,128)S(1)} %get-tuple-element.10.gq, f32[2064,128]{1,0:T(8,128)S(1)} %get-tuple-element.11.gp), custom_call_target="tpu_custom_call" | custom-call | tf_op jit(solution)/shard_map/pallas_call | solution.py:342

commit v6 on v5

--- a/solution.py
+++ b/solution.py
@@ -133,16 +133,7 @@
         vec = op(vec, pltpu.roll(vec, 2, 0))
         return op(vec, pltpu.roll(vec, 4, 0))
 
-    def forward(k, _):
-        @pl.when(k > 0)
-        def _():
-            pltpu.make_async_copy(qbuf.at[k], qbuf.at[k], q_recv.at[k]).wait()
-
-        @pl.when(k == 2)
-        def _():
-            pl.semaphore_wait(column_sem, len(column))
-            vouch(core_sem, core)
-
+    def forward(k):
         q = qbuf[k, pl.ds(0, q_rows), :]
         top = jnp.full((8, q_rows), -jnp.inf, jnp.float32)
         for c in range(CHUNKS):
@@ -163,9 +154,21 @@
             total = total + jnp.sum(e, axis=0)
         totals[k] = total
 
+    def pair(turn, _):
+        for k in (2 * turn + 1, 2 * turn + 2):
+            pltpu.make_async_copy(qbuf.at[k], qbuf.at[k], q_recv.at[k]).wait()
+
+        @pl.when(turn == 0)
+        def _():
+            pl.semaphore_wait(column_sem, len(column))
+            vouch(core_sem, core)
+
+        forward(2 * turn + 1)
+        forward(2 * turn + 2)
         return 0
 
-    lax.fori_loop(0, 5, forward, 0)
+    forward(0)
+    lax.fori_loop(0, 2, pair, 0)
 
     parts = []
     total = [all_rows(totals[k], jnp.add) for k in range(5)]

time: 31.2 us -> 31.1 us (level)
  no operation moved by 1% of the time
where the time goes in v6:
time: 31.1 us; the launch traced here: 31 us
  Pallas kernels  29 us (93%)
  between operations  1.93 us (6%)
    pallas_call x1, Pallas kernels, per_device(): pl.pallas_call(lambda *refs: kernel(n_dev, q_rows, p_rows, *refs), out_sh...  28 us
    pallas_call x1, Pallas kernels, per_device(): pl.pallas_call(finish, out_shape=(jax.ShapeDtypeStruct((1, 1), f32), gq_s...  1.04 us

profile of v6, /device:TPU:1, one launch (start us, length us, event | category | flops | bytes accessed | tf_op | source)
XLA Modules:
  0.0 31.0 jit_solution(16018814514537039704)
XLA Ops:
  1.9 28.0 %shard_map.85 = (f32[1,128]{1,0:T(1,128)S(1)}, f32[256,128]{1,0:T(8,128)S(1)}, f32[2064,128]{1,0:T(8,128)S(1)}) custom-call(bf16[256,128]{1,0:T(8,128)(2,1)} %bitcast.10, bf16[1030,2,128]{2,1,0:T(2,128)(2,1)} %bitcast.9, s32[2]{0:T(128)} %refs_2_.1, s32[8]{0:T(128)} %refs_3_.1, f32[1]{0:T(128)} %bitcast.7.refs_4_, f32[1]{0:T(128)} %bitcast.8.refs_5_), custom_call_target="tpu_custom_call" | custom-call | tf_op jit(solution)/shard_map/pallas_call | solution.py:308
  29.9 1.0 %shard_map.86 = (f32[1,1]{1,0:T(1,128)}, f32[256,128]{1,0:T(8,128)}, f32[1030,2,128]{2,1,0:T(2,128)}) custom-call(f32[1,128]{1,0:T(1,128)S(1)} %get-tuple-element.9.loss, f32[256,128]{1,0:T(8,128)S(1)} %get-tuple-element.10.gq, f32[2064,128]{1,0:T(8,128)S(1)} %get-tuple-element.11.gp), custom_call_target="tpu_custom_call" | custom-call | tf_op jit(solution)/shard_map/pallas_call | solution.py:345

commit v7 on v6

--- a/solution.py
+++ b/solution.py
@@ -36,7 +36,7 @@
     q_hbm, p_hbm, counts_hbm, labels_hbm, scale_hbm, bias_hbm,
     loss_out, gq_out, gp_out,
     counts, labels, scale, bias,
-    qbuf, pg, pgt, xs, tops, totals, factors, gown, gsend, grecv, ones, lsend, l1, l2,
+    qbuf, pg, pgt, xs, tops, totals, factors, losses, gown, gsend, grecv, ones, lsend, l1, l2,
     local_sem, q_send, q_recv, g_send, g_recv, l_send, l_recv, column_sem, core_sem,
 ):
     me = lax.axis_index("dp")
@@ -154,6 +154,35 @@
             total = total + jnp.sum(e, axis=0)
         totals[k] = total
 
+    def scores(blocks):
+        parts = []
+        total = [all_rows(totals[k], jnp.add) for k in blocks]
+        for n, k in enumerate(blocks):
+            soft = tops[k] + TAU * jnp.log(total[n])
+            hi = soft.astype(jnp.bfloat16).astype(jnp.float32)
+            rest = soft - hi
+            mid = rest.astype(jnp.bfloat16).astype(jnp.float32)
+            parts += [hi, mid, rest - mid]
+        if len(parts) % 2:
+            parts.append(jnp.zeros_like(parts[0]))
+        parts = jnp.concatenate(parts, axis=0).astype(jnp.bfloat16)
+        sums = jnp.dot(parts, ones[...], preferred_element_type=jnp.float32).reshape(-1, 8, q_rows)
+        loss = jnp.zeros((8, q_rows), jnp.float32)
+        for n, k in enumerate(blocks):
+            score = sums[3 * n] + sums[3 * n + 1] + sums[3 * n + 2]
+            logit = scale[0] * score + bias[0]
+            tag = qbuf[k, pl.ds(q_rows, 16), :].astype(jnp.float32)
+            block = jnp.concatenate([tag[0:1], tag[1:2]], axis=1)
+            page = jnp.concatenate([tag[2:3], tag[3:4]], axis=1)
+            positive = (block == me.astype(jnp.float32)) & (page == parity.astype(jnp.float32))
+            sign = jnp.where(positive, 1.0, -1.0)
+            t = -sign * logit
+            decay = jnp.exp(-jnp.abs(t))
+            loss = loss + (jnp.maximum(t, 0.0) + jnp.log1p(decay))
+            slope = -sign * scale[0] * jnp.where(t >= 0, 1.0, decay) / (1.0 + decay)
+            factors[k] = slope / total[n]
+        return loss
+
     def pair(turn, _):
         for k in (2 * turn + 1, 2 * turn + 2):
             pltpu.make_async_copy(qbuf.at[k], qbuf.at[k], q_recv.at[k]).wait()
@@ -165,35 +194,12 @@
 
         forward(2 * turn + 1)
         forward(2 * turn + 2)
+        losses[...] += scores((2 * turn + 1, 2 * turn + 2))
         return 0
 
     forward(0)
+    losses[...] = scores((0,))
     lax.fori_loop(0, 2, pair, 0)
-
-    parts = []
-    total = [all_rows(totals[k], jnp.add) for k in range(5)]
-    for k in range(5):
-        soft = tops[k] + TAU * jnp.log(total[k])
-        hi = soft.astype(jnp.bfloat16).astype(jnp.float32)
-        rest = soft - hi
-        mid = rest.astype(jnp.bfloat16).astype(jnp.float32)
-        parts += [hi, mid, rest - mid]
-    parts = jnp.concatenate(parts + [jnp.zeros_like(parts[0])], axis=0).astype(jnp.bfloat16)
-    sums = jnp.dot(parts, ones[...], preferred_element_type=jnp.float32).reshape(16, 8, q_rows)
-    loss = jnp.zeros((8, q_rows), jnp.float32)
-    for k in range(5):
-        score = sums[3 * k] + sums[3 * k + 1] + sums[3 * k + 2]
-        logit = scale[0] * score + bias[0]
-        tag = qbuf[k, pl.ds(q_rows, 16), :].astype(jnp.float32)
-        block = jnp.concatenate([tag[0:1], tag[1:2]], axis=1)
-        page = jnp.concatenate([tag[2:3], tag[3:4]], axis=1)
-        positive = (block == me.astype(jnp.float32)) & (page == parity.astype(jnp.float32))
-        sign = jnp.where(positive, 1.0, -1.0)
-        t = -sign * logit
-        decay = jnp.exp(-jnp.abs(t))
-        loss = loss + (jnp.maximum(t, 0.0) + jnp.log1p(decay))
-        slope = -sign * scale[0] * jnp.where(t >= 0, 1.0, decay) / (1.0 + decay)
-        factors[k] = slope / total[k]
 
     def l_copy(stage, slot):
         return pltpu.make_async_remote_copy(
@@ -217,7 +223,7 @@
             v = v[:half] + v[half:]
         return v[0]
 
-    loss = jnp.sum(loss, axis=0, keepdims=True)
+    loss = jnp.sum(losses[...], axis=0, keepdims=True)
     pl.semaphore_wait(core_sem, len(core))
     l_start(0, loss[:, :EMB] + loss[:, EMB:])
 
@@ -322,6 +328,7 @@
             pltpu.VMEM((5, 8, q_rows), f32),
             pltpu.VMEM((5, 8, q_rows), f32),
             pltpu.VMEM((5, 8, q_rows), f32),
+            pltpu.VMEM((8, q_rows), f32),
             pltpu.VMEM((emb, q_rows), f32),
             pltpu.VMEM((5, emb, q_rows), bf16),
             pltpu.VMEM((5, emb, q_rows), bf16),

time: 31.1 us -> 31 us (level)
  no operation moved by 1% of the time
where the time goes in v7:
time: 31 us; the launch traced here: 30.9 us
  Pallas kernels  29 us (94%)
  between operations  1.93 us (6%)
    pallas_call x1, Pallas kernels, per_device(): pl.pallas_call(lambda *refs: kernel(n_dev, q_rows, p_rows, *refs), out_sh...  27.9 us
    pallas_call x1, Pallas kernels, per_device(): pl.pallas_call(finish, out_shape=(jax.ShapeDtypeStruct((1, 1), f32), gq_s...  1.04 us

profile of v7, /device:TPU:1, one launch (start us, length us, event | category | flops | bytes accessed | tf_op | source)
XLA Modules:
  0.0 30.9 jit_solution(17388156902151257788)
XLA Ops:
  1.9 27.9 %shard_map.85 = (f32[1,128]{1,0:T(1,128)S(1)}, f32[256,128]{1,0:T(8,128)S(1)}, f32[2064,128]{1,0:T(8,128)S(1)}) custom-call(bf16[256,128]{1,0:T(8,128)(2,1)} %bitcast.10, bf16[1030,2,128]{2,1,0:T(2,128)(2,1)} %bitcast.9, s32[2]{0:T(128)} %refs_2_.1, s32[8]{0:T(128)} %refs_3_.1, f32[1]{0:T(128)} %bitcast.7.refs_4_, f32[1]{0:T(128)} %bitcast.8.refs_5_), custom_call_target="tpu_custom_call" | custom-call | tf_op jit(solution)/shard_map/pallas_call | solution.py:314
  29.9 1.0 %shard_map.86 = (f32[1,1]{1,0:T(1,128)}, f32[256,128]{1,0:T(8,128)}, f32[1030,2,128]{2,1,0:T(2,128)}) custom-call(f32[1,128]{1,0:T(1,128)S(1)} %get-tuple-element.9.loss, f32[256,128]{1,0:T(8,128)S(1)} %get-tuple-element.10.gq, f32[2064,128]{1,0:T(8,128)S(1)} %get-tuple-element.11.gp), custom_call_target="tpu_custom_call" | custom-call | tf_op jit(solution)/shard_map/pallas_call | solution.py:352
